TPU v7x, 32 devices: a whole 2x2x4 slice. The times are simulated.
32 devices in a mesh: dp: 8 (over z, y), pix: 4 (over x, core).
Axes of the slice: x: 2, y: 2, z: 4, core: 2. Of those that a mesh axis runs over, the one named last changes fastest.
Arguments:
- latents: bfloat16 [64, 128, 1024], P(('dp', 'pix')), may hold values from -6 to 6
- pixels: bfloat16 [64, 1536, 1024], P('dp', 'pix'), may hold values from -6 to 6
- pixel_mask: int32 [64, 1536], P('dp', 'pix'), may hold values from 0 to 1, as said below
- cotangent: bfloat16 [64, 128, 1024], P(('dp', 'pix')), may hold values from -6 to 6
- lat_gain: float32 [1024], replicated, may hold values from 0.5 to 1.5
- pix_gain: float32 [1024], replicated, may hold values from 0.5 to 1.5
- self_gain: float32 [1024], replicated, may hold values from 0.5 to 1.5
- mlp_gain: float32 [1024], replicated, may hold values from 0.5 to 1.5
- w_query: bfloat16 [1024, 1024], replicated, may hold values from -0.1875 to 0.1875
- w_kv: bfloat16 [1024, 2048], replicated, may hold values from -0.1875 to 0.1875
- w_cross_out: bfloat16 [1024, 1024], replicated, may hold values from -6 to 6
- w_qkv: bfloat16 [1024, 3072], replicated, may hold values from -0.1875 to 0.1875
- w_self_out: bfloat16 [1024, 1024], replicated, may hold values from -1 to 1
- w_mlp_in: bfloat16 [1024, 4096], replicated, may hold values from -0.1875 to 0.1875
- w_mlp_out: bfloat16 [4096, 1024], replicated, may hold values from -0.09375 to 0.09375
Outputs:
- latents_out: bfloat16 [64, 128, 1024], P(('dp', 'pix'))
- d_latents: float32 [64, 128, 1024], P(('dp', 'pix'))
- d_pixels: bfloat16 [64, 1536, 1024], P('dp', 'pix')
- d_lat_gain: float32 [1024], P('dp')
- d_pix_gain: float32 [1024], P('dp')
- d_self_gain: float32 [1024], P('dp')
- d_mlp_gain: float32 [1024], P('dp')
- d_w_query: float32 [1024, 1024], P('dp', 'pix')
- d_w_kv: float32 [1024, 2048], P('dp', 'pix')
- d_w_cross_out: float32 [1024, 1024], P('dp', 'pix')
- d_w_qkv: float32 [1024, 3072], P('dp', 'pix')
- d_w_self_out: float32 [1024, 1024], P('dp', 'pix')
- d_w_mlp_in: float32 [1024, 4096], P('dp', 'pix')
- d_w_mlp_out: float32 [4096, 1024], P('dp', 'pix')
Inputs may be any that keep to these rules, and one draw needn't show every extreme that they name: `pixel_mask`: each group's valid pixel slots are its first n, with n one of 474, 929 or 1536; in every aligned block of 8 groups at least one group has all 1536.
All inputs are finite; a program needn't handle non-finite values.
Results may differ from a plain program's by a relative error of at most 0.028.
Values may be sent and summed in bfloat16 or wider, within the bound.
No kernel may reach another device: no remote copies, remote signals or barrier semaphores. Data moves between devices by JAX's collectives and lax.ppermute only.
A program may use at most 320 MiB of HBM per device.

v0:
```python
import jax
import jax.numpy as jnp
from jax import lax
from jax.sharding import PartitionSpec as P

HEADS = 8


EPSILON = 1e-05


def combined_all(x, axis, join):
    gathered = jax.tree.map(
        lambda a, kind: lax.all_gather(a.astype(kind), axis), x, (jnp.bfloat16, jnp.bfloat16)
    )

    def take(source):
        return jax.tree.map(
            lambda a, own: lax.dynamic_index_in_dim(a, source, 0, False).astype(own.dtype),
            gathered,
            x,
        )

    return lax.fori_loop(
        1, lax.axis_size(axis), lambda source, state: join(state, take(source)), take(0)
    )


def layer_norm(values_in, norm_gain):
    row_mean = jnp.mean(values_in, axis=-1, keepdims=True)
    centred = values_in - row_mean
    row_var = jnp.mean(centred * centred, axis=-1, keepdims=True)
    return centred * lax.rsqrt(row_var + EPSILON) * norm_gain


def exact_gelu(values_in):
    return jax.nn.gelu(values_in, approximate=False)


def combine_stats(earlier, later):
    row_top = jnp.maximum(earlier[0], later[0])
    return (
        row_top,
        earlier[1] * jnp.exp(earlier[0] - row_top) + later[1] * jnp.exp(later[0] - row_top),
    )


def project(left_rows, weight):
    return jnp.einsum("gtd,de->gte", left_rows, weight, preferred_element_type=jnp.float32)


def project_back(grad_low, weight):
    return jnp.einsum("gte,de->gtd", grad_low, weight, preferred_element_type=jnp.float32)


def weight_grad(left_rows, grad_low):
    return jnp.einsum("gtd,gte->de", left_rows, grad_low, preferred_element_type=jnp.float32)


def split_heads(tensor_in, head_count):
    return tensor_in.reshape(
        tensor_in.shape[0], tensor_in.shape[1], head_count, tensor_in.shape[2] // head_count
    )


def join_heads(tensor_in):
    return tensor_in.reshape(
        tensor_in.shape[0], tensor_in.shape[1], tensor_in.shape[2] * tensor_in.shape[3]
    )


def shards(
    latents,
    pixels,
    pixel_mask,
    cotangent,
    lat_gain,
    pix_gain,
    self_gain,
    mlp_gain,
    w_query,
    w_kv,
    w_cross_out,
    w_qkv,
    w_self_out,
    w_mlp_in,
    w_mlp_out,
):
    model_width = pixels.shape[2]
    head_count = HEADS
    score_scale = (model_width // head_count) ** (-0.5)
    mask_rows = pixel_mask.astype(jnp.float32)[:, None, None, :]
    valid_rows = pixel_mask[:, None, None, :] > 0
    lat_float = latents.astype(jnp.float32)
    lat_normed, lat_back = jax.vjp(layer_norm, lat_float, lat_gain)
    lat_low = lat_normed.astype(jnp.bfloat16)
    lat_query = project(lat_low, w_query).astype(jnp.bfloat16)
    query_all = lax.all_gather(lat_query, "pix", axis=0, tiled=True)
    query_heads = split_heads(query_all, head_count)
    pix_normed, pix_back = jax.vjp(layer_norm, pixels.astype(jnp.float32), pix_gain)
    pix_low = pix_normed.astype(jnp.bfloat16)
    key_value = project(pix_low, w_kv).astype(jnp.bfloat16)
    pix_keys = split_heads(key_value[:, :, :model_width], head_count)
    pix_values = split_heads(key_value[:, :, model_width:], head_count)

    def cross_scores():
        raw_scores = (
            jnp.einsum("glhd,gphd->ghlp", query_heads, pix_keys, preferred_element_type=jnp.float32)
            * score_scale
        )
        return jnp.where(valid_rows, raw_scores, -1e30)

    masked = cross_scores()
    local_top = jnp.max(masked, axis=-1)
    local_total = jnp.sum(jnp.exp(masked - local_top[..., None]) * mask_rows, axis=-1)
    row_top, row_total = combined_all((local_top, local_total), "pix", combine_stats)
    cross_weights = (
        jnp.exp(masked - row_top[..., None]) * mask_rows / row_total[..., None]
    ).astype(jnp.bfloat16)
    partial_value = join_heads(
        jnp.einsum("ghlp,gphd->glhd", cross_weights, pix_values, preferred_element_type=jnp.float32)
    )
    cross_mixed = lax.psum_scatter(
        partial_value.astype(jnp.bfloat16), "pix", scatter_dimension=0, tiled=True
    )
    first_sum = lat_float + project(cross_mixed, w_cross_out)
    self_normed, self_back = jax.vjp(layer_norm, first_sum, self_gain)
    self_low = self_normed.astype(jnp.bfloat16)
    self_qkv = project(self_low, w_qkv).astype(jnp.bfloat16)
    self_query = split_heads(self_qkv[:, :, :model_width], head_count)
    self_keys = split_heads(self_qkv[:, :, model_width : 2 * model_width], head_count)
    self_values = split_heads(self_qkv[:, :, 2 * model_width :], head_count)
    self_scores = (
        jnp.einsum("glhd,gmhd->ghlm", self_query, self_keys, preferred_element_type=jnp.float32)
        * score_scale
    )
    self_expo = jnp.exp(self_scores - jnp.max(self_scores, axis=-1, keepdims=True))
    self_probs = self_expo / jnp.sum(self_expo, axis=-1, keepdims=True)
    self_weights = self_probs.astype(jnp.bfloat16)
    inner_low = join_heads(
        jnp.einsum("ghlm,gmhd->glhd", self_weights, self_values, preferred_element_type=jnp.float32)
    ).astype(jnp.bfloat16)
    second = first_sum + project(inner_low, w_self_out)
    mlp_normed, mlp_back = jax.vjp(layer_norm, second, mlp_gain)
    mlp_low = mlp_normed.astype(jnp.bfloat16)
    hidden = project(mlp_low, w_mlp_in)
    activation, gelu_back = jax.vjp(exact_gelu, hidden)
    act_low = activation.astype(jnp.bfloat16)
    latents_out = (second + project(act_low, w_mlp_out)).astype(jnp.bfloat16)
    d_w_mlp_out = weight_grad(act_low, cotangent)
    d_activation = project_back(cotangent, w_mlp_out)
    d_hidden = gelu_back(d_activation)[0].astype(jnp.bfloat16)
    d_w_mlp_in = weight_grad(mlp_low, d_hidden)
    d_second_part, d_mlp_gain = mlp_back(project_back(d_hidden, w_mlp_in))
    d_second = cotangent.astype(jnp.float32) + d_second_part
    d_second_low = d_second.astype(jnp.bfloat16)
    d_w_self_out = weight_grad(inner_low, d_second_low)
    d_inner = split_heads(project_back(d_second_low, w_self_out).astype(jnp.bfloat16), head_count)
    self_dp = jnp.einsum(
        "glhd,gmhd->ghlm", d_inner, self_values, preferred_element_type=jnp.float32
    )
    self_dscores = (
        self_probs * (self_dp - jnp.sum(self_probs * self_dp, axis=-1, keepdims=True))
    ).astype(jnp.bfloat16)
    d_self_query = (
        jnp.einsum("ghlm,gmhd->glhd", self_dscores, self_keys, preferred_element_type=jnp.float32)
        * score_scale
    )
    d_self_keys = (
        jnp.einsum("ghlm,glhd->gmhd", self_dscores, self_query, preferred_element_type=jnp.float32)
        * score_scale
    )
    d_self_values = jnp.einsum(
        "ghlm,glhd->gmhd", self_weights, d_inner, preferred_element_type=jnp.float32
    )
    d_qkv = jnp.concatenate(
        [join_heads(d_self_query), join_heads(d_self_keys), join_heads(d_self_values)], axis=-1
    ).astype(jnp.bfloat16)
    d_w_qkv = weight_grad(self_low, d_qkv)
    d_first_part, d_self_gain = self_back(project_back(d_qkv, w_qkv))
    d_first = d_second + d_first_part
    d_first_low = d_first.astype(jnp.bfloat16)
    d_w_cross_out = weight_grad(cross_mixed, d_first_low)
    d_cross = project_back(d_first_low, w_cross_out).astype(jnp.bfloat16)
    d_cross_all = lax.all_gather(d_cross, "pix", axis=0, tiled=True)
    d_cross_heads = split_heads(d_cross_all, head_count)
    cross_dp = jnp.einsum(
        "glhd,gphd->ghlp", d_cross_heads, pix_values, preferred_element_type=jnp.float32
    )
    cross_probs = jnp.exp(cross_scores() - row_top[..., None]) * mask_rows / row_total[..., None]
    row_delta = lax.psum(
        jnp.sum(cross_probs * cross_dp, axis=-1).astype(jnp.bfloat16), "pix"
    ).astype(jnp.float32)
    cross_dscores = (cross_probs * (cross_dp - row_delta[..., None])).astype(jnp.bfloat16)
    d_query_part = join_heads(
        jnp.einsum("ghlp,gphd->glhd", cross_dscores, pix_keys, preferred_element_type=jnp.float32)
        * score_scale
    )
    d_query = lax.psum_scatter(
        d_query_part.astype(jnp.bfloat16), "pix", scatter_dimension=0, tiled=True
    )
    d_keys = (
        jnp.einsum(
            "ghlp,glhd->gphd", cross_dscores, query_heads, preferred_element_type=jnp.float32
        )
        * score_scale
    )
    d_values = jnp.einsum(
        "ghlp,glhd->gphd",
        cross_probs.astype(jnp.bfloat16),
        d_cross_heads,
        preferred_element_type=jnp.float32,
    )
    d_kv = jnp.concatenate([join_heads(d_keys), join_heads(d_values)], axis=-1).astype(jnp.bfloat16)
    d_w_query = weight_grad(lat_low, d_query)
    d_lat_part, d_lat_gain = lat_back(project_back(d_query, w_query))
    d_latents = d_first + d_lat_part
    d_w_kv = weight_grad(pix_low, d_kv)
    d_pix_float, d_pix_gain = pix_back(project_back(d_kv, w_kv))
    d_pixels = d_pix_float.astype(jnp.bfloat16)
    (
        summed_query,
        summed_kv,
        summed_cross,
        summed_qkv,
        summed_self,
        summed_in,
        summed_out,
        summed_lat,
        summed_pix,
        summed_norm,
        summed_mlp,
    ) = (
        lax.psum_scatter(
            d_w_query.astype(jnp.bfloat16), "dp", scatter_dimension=0, tiled=True
        ).astype(jnp.float32),
        lax.psum_scatter(d_w_kv.astype(jnp.bfloat16), "dp", scatter_dimension=0, tiled=True).astype(
            jnp.float32
        ),
        lax.psum_scatter(
            d_w_cross_out.astype(jnp.bfloat16), "dp", scatter_dimension=0, tiled=True
        ).astype(jnp.float32),
        lax.psum_scatter(
            d_w_qkv.astype(jnp.bfloat16), "dp", scatter_dimension=0, tiled=True
        ).astype(jnp.float32),
        lax.psum_scatter(
            d_w_self_out.astype(jnp.bfloat16), "dp", scatter_dimension=0, tiled=True
        ).astype(jnp.float32),
        lax.psum_scatter(
            d_w_mlp_in.astype(jnp.bfloat16), "dp", scatter_dimension=0, tiled=True
        ).astype(jnp.float32),
        lax.psum_scatter(
            d_w_mlp_out.astype(jnp.bfloat16), "dp", scatter_dimension=0, tiled=True
        ).astype(jnp.float32),
        lax.psum_scatter(
            d_lat_gain.astype(jnp.bfloat16), "dp", scatter_dimension=0, tiled=True
        ).astype(jnp.float32),
        lax.psum_scatter(
            d_pix_gain.astype(jnp.bfloat16), "dp", scatter_dimension=0, tiled=True
        ).astype(jnp.float32),
        lax.psum_scatter(
            d_self_gain.astype(jnp.bfloat16), "dp", scatter_dimension=0, tiled=True
        ).astype(jnp.float32),
        lax.psum_scatter(
            d_mlp_gain.astype(jnp.bfloat16), "dp", scatter_dimension=0, tiled=True
        ).astype(jnp.float32),
    )
    summed_query, summed_kv, summed_cross, summed_qkv, summed_self, summed_in, summed_out = (
        lax.psum_scatter(
            summed_query.astype(jnp.bfloat16), "pix", scatter_dimension=1, tiled=True
        ).astype(jnp.float32),
        lax.psum_scatter(
            summed_kv.astype(jnp.bfloat16), "pix", scatter_dimension=1, tiled=True
        ).astype(jnp.float32),
        lax.psum_scatter(
            summed_cross.astype(jnp.bfloat16), "pix", scatter_dimension=1, tiled=True
        ).astype(jnp.float32),
        lax.psum_scatter(
            summed_qkv.astype(jnp.bfloat16), "pix", scatter_dimension=1, tiled=True
        ).astype(jnp.float32),
        lax.psum_scatter(
            summed_self.astype(jnp.bfloat16), "pix", scatter_dimension=1, tiled=True
        ).astype(jnp.float32),
        lax.psum_scatter(
            summed_in.astype(jnp.bfloat16), "pix", scatter_dimension=1, tiled=True
        ).astype(jnp.float32),
        lax.psum_scatter(
            summed_out.astype(jnp.bfloat16), "pix", scatter_dimension=1, tiled=True
        ).astype(jnp.float32),
    )
    summed_lat, summed_pix, summed_norm, summed_mlp = lax.psum(
        (summed_lat, summed_pix, summed_norm, summed_mlp), "pix"
    )
    return (
        latents_out,
        d_latents,
        d_pixels,
        summed_lat,
        summed_pix,
        summed_norm,
        summed_mlp,
        summed_query,
        summed_kv,
        summed_cross,
        summed_qkv,
        summed_self,
        summed_in,
        summed_out,
    )


def solution(mesh):
    placed = (
        P(("dp", "pix"), None, None),
        P("dp", "pix", None),
        P("dp", "pix"),
        P(("dp", "pix"), None, None),
        P(),
        P(),
        P(),
        P(),
        P(),
        P(),
        P(),
        P(),
        P(),
        P(),
        P(),
    )
    return jax.shard_map(
        shards,
        mesh=mesh,
        in_specs=placed,
        out_specs=(
            P(("dp", "pix"), None, None),
            P(("dp", "pix"), None, None),
            P("dp", "pix", None),
            P("dp"),
            P("dp"),
            P("dp"),
            P("dp"),
            P("dp", "pix"),
            P("dp", "pix"),
            P("dp", "pix"),
            P("dp", "pix"),
            P("dp", "pix"),
            P("dp", "pix"),
            P("dp", "pix"),
        ),
        check_vma=False,
    )
```

profile of v0, /device:TPU:0, one launch (start us, length us, event | category | flops | bytes accessed | tf_op | source)
XLA Modules:
  0.0 1219.1 jit_solution(11116677680030267074)
XLA Ops:
  21.8 16.1 %convolution_convert_fusion = bf16[8,384,2048]{2,1,0:T(8,128)(2,1)} fusion(bf16[1024,2048]{1,0:T(8,128)(2,1)S(1)} %copy-done.51, bf16[8,384,1024]{2,1,0:T(8,128)(2,1)S(1)} %copy-done.3, f32[1024]{0:T(1024)S(1)} %copy-done.42, f32[8,384]{1,0:T(8,128)S(1)} %fusion.124, f32[8,384]{1,0:T(8,128)S(1)} %broadcast_multiply_fusion), kind=kOutput, calls=%fused_computation.42 | convolution fusion | flops 12906921984 | bytes 23097344 | tf_op jit(solution)/shard_map/gtd,de->gte/dot_general | solution.py:49
  37.9 11.3 fusion.136
  49.2 8.6 copy.186
  84.0 11.0 fusion.67
  95.1 33.0 %reduce-scatter.17.cloned.1.call-done = bf16[2,128,1024]{1,2,0:T(8,128)(2,1)} async-done(((bf16[8,128,1024]{1,2,0:T(8,128)(2,1)}), bf16[2,128,1024]{1,2,0:T(8,128)(2,1)}) %reduce-scatter.17.cloned.1.call-update) | async-done | bytes 524304 | tf_op jit(solution)/shard_map/reduce_scatter | solution.py:123
  153.7 10.6 multiply_convert_fusion.3
  164.4 8.5 add_convert_fusion.1
  203.4 22.7 %all-gather.7.cloned.1.call-done = bf16[8,128,1024]{2,1,0:T(8,128)(2,1)} async-done(((bf16[2,128,1024]{2,1,0:T(8,128)(2,1)}), bf16[8,128,1024]{2,1,0:T(8,128)(2,1)}) %all-gather.7.cloned.1.call-update) | async-done | bytes 2097168 | tf_op jit(solution)/shard_map/all_gather | solution.py:185
  229.9 12.9 %multiply_reduce_fusion = (bf16[8,8,128]{2,1,0:T(8,128)(2,1)S(1)}, f32[8,8,128,384]{3,2,1,0:T(8,128)}) fusion(f32[8,8,128]{2,1,0:T(8,128)S(1)} %get-tuple-element.148, f32[8,384]{1,0:T(8,128)S(1)} %convert_element_type.259, f32[8,8,128]{2,1,0:T(8,128)S(1)} %get-tuple-element.147, f32[8,8,128,384]{3,2,1,0:T(8,128)} %copy-done.2, ...), kind=kOutput, calls=%fused_computation.26 | convolution fusion | flops 827318272 | bytes 33651712 | tf_op jit(solution)/shard_map/glhd,gphd->ghlp/dot_general | solution.py:187
  242.9 10.2 psum.35
  253.1 11.6 multiply_convert_fusion.1
  264.6 9.1 multiply_convert_fusion.2
  283.2 27.2 %reduce-scatter.19.cloned.1.call-done = bf16[2,128,1024]{2,1,0:T(8,128)(2,1)} async-done(((bf16[8,128,1024]{2,1,0:T(8,128)(2,1)}), bf16[2,128,1024]{2,1,0:T(8,128)(2,1)}) %reduce-scatter.19.cloned.1.call-update) | async-done | bytes 524304 | tf_op jit(solution)/shard_map/reduce_scatter | solution.py:199
  313.8 9.7 convolution_convert_fusion.1
  323.5 8.8 copy.165
  339.7 8.7 copy.164
  348.4 22.1 %bitcast_convert_fusion.3 = bf16[1024,2048]{1,0:T(8,128)(2,1)} fusion(bf16[8,384,1024]{2,1,0:T(8,128)(2,1)} %copy.165, bf16[8,384,1024]{2,1,0:T(8,128)(2,1)} %copy.164, bf16[8,384,1024]{2,1,0:T(8,128)(2,1)} %param.18, f32[1024]{0:T(1024)S(1)} %copy-done.43, f32[8,384]{1,0:T(8,128)S(1)} %copy-done.34, f32[8,384]{1,0:T(8,128)S(1)} %copy-done.32), kind=kOutput, calls=%fused_computation.31 | convolution fusion | flops 12927893504 | bytes 23097344 | tf_op jit(solution)/shard_map/gtd,gte->de/dot_general | solution.py:57
  394.0 57.8 %reduce-scatter.37.cloned.1.call-done = bf16[128,1024]{1,0:T(8,128)(2,1)} async-done(((bf16[1024,1024]{1,0:T(8,128)(2,1)}), bf16[128,1024]{1,0:T(8,128)(2,1)}) %reduce-scatter.37.cloned.1.call-update) | async-done | bytes 262160 | tf_op jit(solution)/shard_map/reduce_scatter | solution.py:246
  451.9 70.4 %reduce-scatter.21.cloned.1.call-done = bf16[128,1024]{1,0:T(8,128)(2,1)} async-done(((bf16[1024,1024]{1,0:T(8,128)(2,1)}), bf16[128,1024]{1,0:T(8,128)(2,1)}) %reduce-scatter.21.cloned.1.call-update) | async-done | bytes 262160 | tf_op jit(solution)/shard_map/reduce_scatter | solution.py:234
  522.4 90.5 %reduce-scatter.25.cloned.1.call-done = bf16[128,2048]{1,0:T(8,128)(2,1)} async-done(((bf16[1024,2048]{1,0:T(8,128)(2,1)}), bf16[128,2048]{1,0:T(8,128)(2,1)}) %reduce-scatter.25.cloned.1.call-update) | async-done | bytes 524304 | tf_op jit(solution)/shard_map/reduce_scatter | solution.py:237
  612.9 122.2 %reduce-scatter.33.cloned.1.call-done = bf16[128,3072]{1,0:T(8,128)(2,1)} async-done(((bf16[1024,3072]{1,0:T(8,128)(2,1)}), bf16[128,3072]{1,0:T(8,128)(2,1)}) %reduce-scatter.33.cloned.1.call-update) | async-done | bytes 786448 | tf_op jit(solution)/shard_map/reduce_scatter | solution.py:243
  743.6 143.7 %reduce-scatter.41.cloned.1.call-done = bf16[128,4096]{1,0:T(8,128)(2,1)} async-done(((bf16[1024,4096]{1,0:T(8,128)(2,1)}), bf16[128,4096]{1,0:T(8,128)(2,1)}) %reduce-scatter.41.cloned.1.call-update) | async-done | bytes 1048592 | tf_op jit(solution)/shard_map/reduce_scatter | solution.py:249
  887.5 21.9 %fusion.13 = (f32[8,384]{1,0:T(8,128)S(1)}, f32[8,384,1024]{2,1,0:T(8,128)}) fusion(bf16[8,384,1024]{2,1,0:T(8,128)(2,1)} %param.18, f32[1024]{0:T(1024)S(1)} %copy-done.43, f32[8,384]{1,0:T(8,128)S(1)} %copy-done.32, bf16[1024,2048]{1,0:T(8,128)(2,1)} %param.26, bf16[8,384,1024]{2,1,0:T(8,128)(2,1)} %copy.165, bf16[8,384,1024]{2,1,0:T(8,128)(2,1)} %copy.164), kind=kOutput, calls=%fused_computation.20 | convolution fusion | flops 12925793280 | bytes 35680256 | tf_op jit(solution)/shard_map/gte,de->gtd/dot_general | solution.py:53
  909.4 9.7 fusion.11
  919.1 119.9 %reduce-scatter.45.cloned.1.call-done = bf16[512,1024]{1,0:T(8,128)(2,1)} async-done(((bf16[4096,1024]{1,0:T(8,128)(2,1)}), bf16[512,1024]{1,0:T(8,128)(2,1)}) %reduce-scatter.45.cloned.1.call-update) | async-done | bytes 1048592 | tf_op jit(solution)/shard_map/reduce_scatter | solution.py:252
  1039.0 11.4 add_convert_fusion
  1050.5 10.0 reduce-scatter.31.cloned.1.call-done
  1062.0 21.0 %reduce-scatter.39.cloned.1.call-done = bf16[128,256]{1,0:T(8,128)(2,1)} async-done(((bf16[128,1024]{1,0:T(8,128)(2,1)}), bf16[128,256]{1,0:T(8,128)(2,1)}) %reduce-scatter.39.cloned.1.call-update) | async-done | bytes 65552 | tf_op jit(solution)/shard_map/reduce_scatter | solution.py:281
  1088.7 21.6 %all-reduce.5 = (bf16[1024]{0:T(1024)(128)(2,1)S(1)}, bf16[1024]{0:T(1024)(128)(2,1)S(1)}, bf16[1024]{0:T(1024)(128)(2,1)S(1)}, bf16[1024]{0:T(1024)(128)(2,1)S(1)}) all-reduce(bf16[1024]{0:T(1024)(128)(2,1)S(1)} %get-tuple-element.157, bf16[1024]{0:T(1024)(128)(2,1)S(1)} %get-tuple-element.149, ...), channel_id=6, replica_groups=mesh['dp'=8,'pix'=4] {'dp'}, use_global_device_ids=true, to_apply=%region_28.29.clone | all-reduce | flops 4096 | bytes 16384
  1131.3 24.2 %reduce-scatter.35.cloned.1.call-done = bf16[128,768]{1,0:T(8,128)(2,1)} async-done(((bf16[128,3072]{1,0:T(8,128)(2,1)}), bf16[128,768]{1,0:T(8,128)(2,1)}) %reduce-scatter.35.cloned.1.call-update) | async-done | bytes 196624 | tf_op jit(solution)/shard_map/reduce_scatter | solution.py:278
  1157.2 25.6 %reduce-scatter.43.cloned.1.call-done = bf16[128,1024]{1,0:T(8,128)(2,1)} async-done(((bf16[128,4096]{1,0:T(8,128)(2,1)}), bf16[128,1024]{1,0:T(8,128)(2,1)}) %reduce-scatter.43.cloned.1.call-update) | async-done | bytes 262160 | tf_op jit(solution)/shard_map/reduce_scatter | solution.py:284
  1184.6 25.7 %reduce-scatter.47.cloned.1.call-done = bf16[512,256]{1,0:T(8,128)(2,1)} async-done(((bf16[512,1024]{1,0:T(8,128)(2,1)}), bf16[512,256]{1,0:T(8,128)(2,1)}) %reduce-scatter.47.cloned.1.call-update) | async-done | bytes 262160 | tf_op jit(solution)/shard_map/reduce_scatter | solution.py:287
  (236 shorter events, 185.7 us)
Async XLA Ops:
  7.2 138.3 %copy-start = (bf16[1024,1024]{1,0:T(8,128)(2,1)S(1)}, bf16[1024,1024]{1,0:T(8,128)(2,1)}, u32[]{:S(2)}) copy-start(bf16[1024,1024]{1,0:T(8,128)(2,1)} %param.29) | copy-start | bytes 6291460
  7.2 50.6 %all-gather.5.cloned.1.call-start = ((), (), s32[]{:S(2)}) async-start(), calls=%async_computation.16 | async-start | bytes 2621440 | tf_op jit(solution)/shard_map/all_gather | solution.py:98
  14.5 113.7 %reduce-scatter.17.cloned.1.call-start = ((), (), s32[]{:S(2)}) async-start(), calls=%async_computation.17 | async-start | bytes 2621440 | tf_op jit(solution)/shard_map/reduce_scatter | solution.py:123
  95.0 36.0 %copy-start.46 = (f32[1024]{0:T(1024)S(1)}, f32[1024]{0:T(1024)}, u32[]{:S(2)}) copy-start(f32[1024]{0:T(1024)} %param.23) | copy-start | bytes 12292
  95.0 131.0 %all-gather.7.cloned.1.call-start = ((), (), s32[]{:S(2)}) async-start(), calls=%async_computation.18 | async-start | bytes 2621440 | tf_op jit(solution)/shard_map/all_gather | solution.py:185
  146.3 33.8 %copy-start.6 = (f32[2,128,1024]{2,1,0:T(8,128)}, f32[2,128,1024]{2,1,0:T(8,128)S(1)}, u32[]{:S(2)}) copy-start(f32[2,128,1024]{2,1,0:T(8,128)S(1)} %get-tuple-element.195) | copy-start | bytes 3145732
  201.7 76.1 %copy-start.10 = (f32[2,128,1024]{2,1,0:T(8,128)}, f32[2,128,1024]{2,1,0:T(8,128)S(1)}, u32[]{:S(2)}) copy-start(f32[2,128,1024]{2,1,0:T(8,128)S(1)} %add_add_fusion.5) | copy-start | bytes 3145732
  203.3 107.1 %reduce-scatter.19.cloned.1.call-start = ((), (), s32[]{:S(2)}) async-start(), calls=%async_computation.19 | async-start | bytes 2621440 | tf_op jit(solution)/shard_map/reduce_scatter | solution.py:199
  277.8 115.7 %reduce-scatter.29.cloned.1.call-start = ((), (), s32[]{:S(2)}) async-start(), calls=%async_computation.24 | async-start | bytes 2359296 | tf_op jit(solution)/shard_map/reduce_scatter | solution.py:240
  279.9 30.5 %copy-start.39 = (f32[1024]{0:T(1024)S(1)}, f32[1024]{0:T(1024)}, u32[]{:S(2)}) copy-start(f32[1024]{0:T(1024)} %param.21) | copy-start | bytes 12292
  279.9 30.5 %copy-start.41 = (f32[2,128]{1,0:T(2,128)S(1)}, f32[2,128]{1,0:T(2,128)}, u32[]{:S(2)}) copy-start(f32[2,128]{1,0:T(2,128)} %copy-done.40) | copy-start | bytes 3076
  279.9 30.5 %copy-start.45 = (f32[2,128]{1,0:T(2,128)S(1)}, f32[2,128]{1,0:T(2,128)}, u32[]{:S(2)}) copy-start(f32[2,128]{1,0:T(2,128)} %copy-done.44) | copy-start | bytes 3076
  279.9 171.9 %reduce-scatter.37.cloned.1.call-start = ((), (), s32[]{:S(2)}) async-start(), calls=%async_computation.28 | async-start | bytes 2359296 | tf_op jit(solution)/shard_map/reduce_scatter | solution.py:246
  283.2 239.1 %reduce-scatter.21.cloned.1.call-start = ((), (), s32[]{:S(2)}) async-start(), calls=%async_computation.20 | async-start | bytes 2359296 | tf_op jit(solution)/shard_map/reduce_scatter | solution.py:234
  313.7 299.1 %reduce-scatter.25.cloned.1.call-start = ((), (), s32[]{:S(2)}) async-start(), calls=%async_computation.22 | async-start | bytes 4718592 | tf_op jit(solution)/shard_map/reduce_scatter | solution.py:237
  370.6 364.5 %reduce-scatter.33.cloned.1.call-start = ((), (), s32[]{:S(2)}) async-start(), calls=%async_computation.26 | async-start | bytes 7077888 | tf_op jit(solution)/shard_map/reduce_scatter | solution.py:243
  376.6 510.6 %reduce-scatter.41.cloned.1.call-start = ((), (), s32[]{:S(2)}) async-start(), calls=%async_computation.30 | async-start | bytes 9437184 | tf_op jit(solution)/shard_map/reduce_scatter | solution.py:249
  385.2 653.8 %reduce-scatter.45.cloned.1.call-start = ((), (), s32[]{:S(2)}) async-start(), calls=%async_computation.32 | async-start | bytes 9437184 | tf_op jit(solution)/shard_map/reduce_scatter | solution.py:252
  393.4 341.9 %copy-start.52 = (u32[32]{0:T(128)S(1)}, u32[32]{0:T(128)}, u32[]{:S(2)}) copy-start(u32[32]{0:T(128)} %constant.150) | copy-start | bytes 388
  393.4 667.1 %reduce-scatter.31.cloned.1.call-start = ((), (), s32[]{:S(2)}) async-start(), calls=%async_computation.25 | async-start | bytes 327680 | tf_op jit(solution)/shard_map/reduce_scatter | solution.py:275
  394.0 689.1 %reduce-scatter.39.cloned.1.call-start = ((), (), s32[]{:S(2)}) async-start(), calls=%async_computation.29 | async-start | bytes 327680 | tf_op jit(solution)/shard_map/reduce_scatter | solution.py:281
  451.8 668.0 %reduce-scatter.23.cloned.1.call-start = ((), (), s32[]{:S(2)}) async-start(), calls=%async_computation.21 | async-start | bytes 327680 | tf_op jit(solution)/shard_map/reduce_scatter | solution.py:269
  522.3 607.3 %reduce-scatter.27.cloned.1.call-start = ((), (), s32[]{:S(2)}) async-start(), calls=%async_computation.23 | async-start | bytes 655360 | tf_op jit(solution)/shard_map/reduce_scatter | solution.py:272
  612.9 542.6 %reduce-scatter.35.cloned.1.call-start = ((), (), s32[]{:S(2)}) async-start(), calls=%async_computation.27 | async-start | bytes 983040 | tf_op jit(solution)/shard_map/reduce_scatter | solution.py:278
  735.2 447.6 %reduce-scatter.43.cloned.1.call-start = ((), (), s32[]{:S(2)}) async-start(), calls=%async_computation.31 | async-start | bytes 1310720 | tf_op jit(solution)/shard_map/reduce_scatter | solution.py:284
  887.3 322.9 %reduce-scatter.47.cloned.1.call-start = ((), (), s32[]{:S(2)}) async-start(), calls=%async_computation.33 | async-start | bytes 1310720 | tf_op jit(solution)/shard_map/reduce_scatter | solution.py:287
  1039.0 45.6 %copy-start.9 = (bf16[2,128,1024]{2,1,0:T(8,128)(2,1)S(1)}, bf16[2,128,1024]{2,1,0:T(8,128)(2,1)}, u32[]{:S(2)}) copy-start(bf16[2,128,1024]{2,1,0:T(8,128)(2,1)} %param.17) | copy-start | bytes 1572868
  1039.0 45.5 %copy-start.29 = (bf16[2,128,1024]{2,1,0:T(8,128)(2,1)S(1)}, bf16[2,128,1024]{2,1,0:T(8,128)(2,1)}, u32[]{:S(2)}) copy-start(bf16[2,128,1024]{2,1,0:T(8,128)(2,1)} %reduce-scatter.19.cloned.1.call-done) | copy-start | bytes 1572868
  1050.5 36.7 %copy-start.48 = (f32[2,128]{1,0:T(2,128)S(1)}, f32[2,128]{1,0:T(2,128)}, u32[]{:S(2)}) copy-start(f32[2,128]{1,0:T(2,128)} %copy-done.47) | copy-start | bytes 3076
  1050.5 38.2 %copy-start.49 = (bf16[1024]{0:T(1024)(128)(2,1)S(1)}, bf16[1024]{0:T(1024)(128)(2,1)}, u32[]{:S(2)}) copy-start(bf16[1024]{0:T(1024)(128)(2,1)} %get-tuple-element.153) | copy-start | bytes 6148
  1050.5 38.2 %copy-start.50 = (bf16[1024]{0:T(1024)(128)(2,1)S(1)}, bf16[1024]{0:T(1024)(128)(2,1)}, u32[]{:S(2)}) copy-start(bf16[1024]{0:T(1024)(128)(2,1)} %get-tuple-element.155) | copy-start | bytes 6148
  1084.6 127.5 %copy-start.1 = (bf16[1024,1024]{1,0:T(8,128)(2,1)S(1)}, bf16[1024,1024]{1,0:T(8,128)(2,1)}, u32[]{:S(2)}) copy-start(bf16[1024,1024]{1,0:T(8,128)(2,1)} %param.29) | copy-start | bytes 6291460
  (39 other events, 234.3 us)
Sparse Core Ops, SparseCore 0:
  14.6 25.2 all-gather.4
  95.2 32.9 reduce-scatter.16
  203.4 22.5 all-gather.6
  277.9 32.4 reduce-scatter.18
  313.8 67.8 reduce-scatter.28
  385.1 66.6 reduce-scatter.36
  455.3 66.9 reduce-scatter.20
  525.9 86.8 reduce-scatter.24
  617.4 117.6 reduce-scatter.32
  739.1 148.1 reduce-scatter.40
  890.9 148.0 reduce-scatter.44
  1041.5 19.0 reduce-scatter.30
  1063.0 20.0 reduce-scatter.38
  1085.5 20.0 reduce-scatter.22
  1107.9 21.6 reduce-scatter.26
  1132.2 23.2 reduce-scatter.34
  1157.9 24.8 reduce-scatter.42
  1185.4 24.8 reduce-scatter.46
where the time goes:
time: 1230 us; the launch traced here: 1220 us
  waiting for transfers between devices  803 us (65%)
  matrix products  206 us (17%)
  other arithmetic  73.8 us (6%)
  local copies, waits for them, and re-layouts  68.6 us (6%)
  blocking collectives  50.2 us (4%)
  between operations  15.8 us (1%)
    reduce_scatter x1, waiting for transfers between devices, shards(): lax.psum_scatter(d_w_mlp_in.astype(jnp.bfloat16), 'dp', scatter_dimension...  144 us
    reduce_scatter x1, waiting for transfers between devices, shards(): lax.psum_scatter(d_w_qkv.astype(jnp.bfloat16), 'dp', scatter_dimension=0,...  122 us
    reduce_scatter x1, waiting for transfers between devices, shards(): lax.psum_scatter(d_w_mlp_out.astype(jnp.bfloat16), 'dp', scatter_dimensio...  120 us
    reduce_scatter x1, waiting for transfers between devices, shards(): lax.psum_scatter(d_w_kv.astype(jnp.bfloat16), 'dp', scatter_dimension=0,...  90.5 us
    reduce_scatter x1, waiting for transfers between devices, shards(): lax.psum_scatter(d_w_query.astype(jnp.bfloat16), 'dp', scatter_dimension=...  70.4 us
    reduce_scatter x1, waiting for transfers between devices, shards(): lax.psum_scatter(d_w_self_out.astype(jnp.bfloat16), 'dp', scatter_dimensi...  57.8 us
    dot_general x7, matrix products, weight_grad(): jnp.einsum('gtd,gte->de', left_rows, grad_low, preferred_element_type=jnp...  49.8 us
    dot_general x7, matrix products, project_back(): jnp.einsum('gte,de->gtd', grad_low, weight, preferred_element_type=jnp.fl...  48.6 us
  transfers between devices with their start and end apart: 18, of which 15 were waited for; matrix products, arithmetic and copies ran while one was open for 16% of the time, Pallas kernels for 0%

commit v1 on v0

v1 whole, which is shorter than its diff:
```python
import functools

import jax
import jax.numpy as jnp
from jax import lax
from jax.experimental import pallas as pl
from jax.experimental.pallas import tpu as pltpu
from jax.sharding import PartitionSpec as P

HEADS = 8
EPSILON = 1e-05
LANES = 128
EMPTY = -1e30
F32 = jnp.float32
BF16 = jnp.bfloat16
NN = (((1,), (0,)), ((), ()))
NT = (((1,), (1,)), ((), ()))
TN = (((0,), (0,)), ((), ()))
ANY = pl.BlockSpec(memory_space=pl.ANY)
MIB = 1024 * 1024


def grid_sizes():
    pix_size = lax.axis_size("pix")
    dp_size = lax.axis_size("dp")
    slow = 4 if dp_size % 4 == 0 else 1
    return {"c": 2, "x": pix_size // 2, "a": slow, "b": dp_size // slow}


def direction(label):
    axis = "pix" if label in "cx" else "dp"
    here = lax.axis_index(axis)
    inner = 2 if axis == "pix" else grid_sizes()["b"]
    if label in "cb":
        return axis, lax.rem(here, inner), 1
    return axis, here // inner, inner


def move(value, label, moves):
    sizes = grid_sizes()
    axis, _, stride = direction(label)
    other = {"c": "x", "x": "c", "a": "b", "b": "a"}[label]
    other_stride = sizes[label] if stride == 1 else 1
    pairs = [
        (src * stride + rest * other_stride, dst * stride + rest * other_stride)
        for rest in range(sizes[other])
        for src, dst in moves
    ]
    return lax.ppermute(value, axis, pairs)


def from_core(value):
    return move(value, "c", [(0, 1), (1, 0)])


def from_x(value, turn):
    size = grid_sizes()["x"]
    return move(value, "x", [((p + turn) % size, p) for p in range(size)])


def add_low(*terms):
    total = terms[0].astype(F32)
    for term in terms[1:]:
        total = total + term.astype(F32)
    return total.astype(terms[0].dtype)


def take_part(parts, index):
    return lax.dynamic_index_in_dim(parts, index, 0, keepdims=False)


def chain_reduce(parts, label):
    size = grid_sizes()[label]
    if size == 1:
        return parts[0]
    _, here, _ = direction(label)
    mine = take_part(parts, here)
    if size == 2:
        return add_low(mine, move(take_part(parts, 1 - here), label, [(0, 1), (1, 0)]))
    up = down = None
    for step in range(1, size):
        up_own = take_part(parts, jnp.clip(size - step + here, 0, size - 1))
        down_own = take_part(parts, jnp.clip(here - (size - step), 0, size - 1))
        up_sent = up_own if up is None else add_low(up_own, up)
        down_sent = down_own if down is None else add_low(down_own, down)
        up = move(up_sent, label, [(p, p + 1) for p in range(step)])
        down = move(down_sent, label, [(size - 1 - p, size - 2 - p) for p in range(step)])
    return add_low(mine, up, down)


def reduce_parts(parts, order):
    for label in order:
        parts = chain_reduce(parts, label)
    return parts.astype(F32)


def everywhere(value, label):
    size = grid_sizes()[label]
    total = value
    for turn in range(1, size):
        total = total + move(value, label, [(p, (p + turn) % size) for p in range(size)])
    return total


def reduce_gains(grads):
    sizes = grid_sizes()
    parts = grads.reshape(grads.shape[0], sizes["a"], sizes["b"], -1).transpose(2, 1, 0, 3)
    total = chain_reduce(chain_reduce(parts, "b"), "a")
    return everywhere(everywhere(total, "c"), "x")


def dot(left, right, dims=NN):
    return lax.dot_general(left, right, dims, preferred_element_type=F32)


def normalize(values):
    centred = values - jnp.mean(values, axis=-1, keepdims=True)
    root = lax.rsqrt(jnp.mean(centred * centred, axis=-1, keepdims=True) + EPSILON)
    return centred * root, root


def norm_low(values, gain):
    return (normalize(values)[0] * gain).astype(BF16)


def norm_back(values, gain, grad):
    hat, root = normalize(values)
    scaled = grad * gain
    along = jnp.mean(scaled * hat, axis=-1, keepdims=True)
    back = root * (scaled - jnp.mean(scaled, axis=-1, keepdims=True) - hat * along)
    parts = grad * hat
    return back, parts.reshape(parts.shape[0] // 8, 8, parts.shape[1]).sum(0)


def pack_stat(stat):
    lane = lax.broadcasted_iota(jnp.int32, stat.shape, 1)
    high = stat.astype(BF16).astype(F32)
    middle = (stat - high).astype(BF16).astype(F32)
    low = stat - high - middle
    packed = jnp.where(lane < HEADS, high, pltpu.roll(middle, HEADS, 1))
    packed = jnp.where(lane < 2 * HEADS, packed, pltpu.roll(low, 2 * HEADS, 1))
    return jnp.where(lane < 3 * HEADS, packed, 0.0)


def unpack_stat(packed):
    full = packed.astype(F32)
    return (
        full + pltpu.roll(full, LANES - HEADS, 1) + pltpu.roll(full, LANES - 2 * HEADS, 1)
    )


def head(index, base=0):
    return slice(base + index * LANES, base + (index + 1) * LANES)


def merge(first, second, width):
    first_stat = unpack_stat(first[:, width:])
    second_stat = unpack_stat(second[:, width:])
    top = jnp.maximum(first_stat, second_stat)
    first_weight = jnp.exp(first_stat - top)
    second_weight = jnp.exp(second_stat - top)
    total = first_weight + second_weight
    first_weight = first_weight / total
    second_weight = second_weight / total
    mixed = [
        first[:, head(h)].astype(F32) * first_weight[:, h : h + 1]
        + second[:, head(h)].astype(F32) * second_weight[:, h : h + 1]
        for h in range(HEADS)
    ]
    return mixed, top + jnp.log(total)


def params(limit=56):
    return pltpu.CompilerParams(vmem_limit_bytes=limit * MIB)


def cost(flops, moved, exps=0):
    return pl.CostEstimate(flops=int(flops), bytes_accessed=int(moved), transcendentals=int(exps))


def shape_of(shape, dtype):
    return jax.ShapeDtypeStruct(shape, dtype)


def pix_project_kernel(pix_ref, gain_ref, weight_ref, low_ref, kv_ref):
    low = norm_low(pix_ref[...].astype(F32), gain_ref[...])
    low_ref[...] = low
    kv_ref[...] = dot(low, weight_ref[...]).astype(BF16)


def pix_project(pixels, gain, weight):
    rows, width = pixels.shape
    wide = weight.shape[1]
    block = 384 if rows % 384 == 0 else 128
    return pl.pallas_call(
        pix_project_kernel,
        grid=(rows // block,),
        in_specs=[
            pl.BlockSpec((block, width), lambda i: (i, 0)),
            pl.BlockSpec((1, width), lambda i: (0, 0)),
            pl.BlockSpec((width, wide), lambda i: (0, 0)),
        ],
        out_specs=[
            pl.BlockSpec((block, width), lambda i: (i, 0)),
            pl.BlockSpec((block, wide), lambda i: (i, 0)),
        ],
        out_shape=[shape_of((rows, width), BF16), shape_of((rows, wide), BF16)],
        compiler_params=params(),
        cost_estimate=cost(2 * rows * width * wide, 2 * rows * (2 * width + wide)),
        name="pix_project",
    )(pixels, gain, weight)


def cross_forward_kernel(group_ref, count_ref, query_ref, kv_ref, out_ref):
    count = count_ref[group_ref[pl.program_id(0)]]
    rows, width = query_ref.shape[1:]
    slots = kv_ref.shape[1]
    valid = lax.broadcasted_iota(jnp.int32, (1, slots), 1) < count
    lane = lax.broadcasted_iota(jnp.int32, (rows, LANES), 1)
    stat = jnp.zeros((rows, LANES), F32)
    for h in range(HEADS):
        scores = dot(query_ref[0, :, head(h)], kv_ref[0, :, head(h)], NT) * LANES**-0.5
        scores = jnp.where(valid, scores, EMPTY)
        top = jnp.max(scores, axis=-1, keepdims=True)
        expo = jnp.where(valid, jnp.exp(scores - top), 0.0)
        total = jnp.sum(expo, axis=-1, keepdims=True)
        mixed = dot(expo.astype(BF16), kv_ref[0, :, head(h, width)])
        some = total > 0.0
        safe = jnp.where(some, total, 1.0)
        out_ref[0, :, head(h)] = (mixed / safe).astype(BF16)
        stat = jnp.where(lane == h, jnp.where(some, top + jnp.log(safe), EMPTY), stat)
    out_ref[0, :, width:] = pack_stat(stat).astype(BF16)


def cross_forward(groups, counts, query, kv):
    number, rows, width = query.shape
    slots, wide = kv.shape[1:]
    return pl.pallas_call(
        cross_forward_kernel,
        grid_spec=pltpu.PrefetchScalarGridSpec(
            num_scalar_prefetch=2,
            grid=(number,),
            in_specs=[
                pl.BlockSpec((1, rows, width), lambda i, g, n: (i, 0, 0)),
                pl.BlockSpec((1, slots, wide), lambda i, g, n: (g[i], 0, 0)),
            ],
            out_specs=pl.BlockSpec((1, rows, width + LANES), lambda i, g, n: (i, 0, 0)),
        ),
        out_shape=shape_of((number, rows, width + LANES), BF16),
        compiler_params=params(),
        cost_estimate=cost(
            8 * number * rows * width * slots, 2 * number * slots * wide, number * rows * HEADS * slots
        ),
        name="cross_forward",
    )(groups, counts, query, kv)


def merge_kernel(first_ref, second_ref, out_ref):
    width = out_ref.shape[2] - LANES
    mixed, stat = merge(first_ref[0], second_ref[0], width)
    for h in range(HEADS):
        out_ref[0, :, head(h)] = mixed[h].astype(BF16)
    out_ref[0, :, width:] = pack_stat(stat).astype(BF16)


def merge_call(first, second):
    number, rows, wide = first.shape
    spec = pl.BlockSpec((1, rows, wide), lambda i: (i, 0, 0))
    return pl.pallas_call(
        merge_kernel,
        grid=(number,),
        in_specs=[spec, spec],
        out_specs=spec,
        out_shape=shape_of(first.shape, BF16),
        compiler_params=params(),
        cost_estimate=cost(8 * number * rows * wide, 6 * number * rows * wide),
        name="merge",
    )(first, second)


def cross_backward_kernel(group_ref, count_ref, query_ref, grad_ref, kv_ref, old_ref, dq_ref, dkv_ref):
    del old_ref
    count = count_ref[group_ref[pl.program_id(0)]]
    width = query_ref.shape[2]
    slots = kv_ref.shape[1]
    valid = lax.broadcasted_iota(jnp.int32, (slots, 1), 0) < count
    stat = grad_ref[0, :, width:].astype(F32).T
    pieces = [stat[HEADS * i : HEADS * (i + 1)] for i in range(6)]
    log_total = pieces[0] + pieces[1] + pieces[2]
    delta = pieces[3] + pieces[4] + pieces[5]
    scale = LANES**-0.5
    for h in range(HEADS):
        query = query_ref[0, :, head(h)]
        grad = grad_ref[0, :, head(h)]
        keys = kv_ref[0, :, head(h)]
        scores = dot(keys, query, NT) * scale - log_total[h : h + 1]
        probs = jnp.where(valid, jnp.exp(scores), 0.0)
        d_probs = dot(kv_ref[0, :, head(h, width)], grad, NT)
        d_scores = (probs * (d_probs - delta[h : h + 1])).astype(BF16)
        dkv_ref[0, :, head(h)] = (dot(d_scores, query) * scale).astype(BF16)
        dkv_ref[0, :, head(h, width)] = dot(probs.astype(BF16), grad).astype(BF16)
        dq_ref[0, :, head(h)] = (dot(d_scores, keys, TN) * scale).astype(BF16)


def cross_backward(groups, counts, query, grad, kv, old):
    number, rows, width = query.shape
    slots, wide = kv.shape[1:]
    first = old is None
    return pl.pallas_call(
        cross_backward_kernel,
        grid_spec=pltpu.PrefetchScalarGridSpec(
            num_scalar_prefetch=2,
            grid=(number,),
            in_specs=[
                pl.BlockSpec((1, rows, width), lambda i, g, n: (i, 0, 0)),
                pl.BlockSpec((1, rows, width + LANES), lambda i, g, n: (i, 0, 0)),
                pl.BlockSpec((1, slots, wide), lambda i, g, n: (g[i], 0, 0)),
                ANY,
            ],
            out_specs=[
                pl.BlockSpec((1, rows, width), lambda i, g, n: (i, 0, 0)),
                pl.BlockSpec((1, slots, wide), lambda i, g, n: (g[i], 0, 0)),
            ],
        ),
        out_shape=[shape_of((number, rows, width), BF16), shape_of(kv.shape, BF16)],
        input_output_aliases={} if first else {5: 1},
        compiler_params=params(),
        cost_estimate=cost(
            10 * number * rows * width * slots, 4 * number * slots * wide, number * rows * HEADS * slots
        ),
        name="cross_backward",
    )(groups, counts, query, grad, kv, counts if first else old)


def pix_back_kernel(dkv_ref, weight_ref, pix_ref, gain_ref, out_ref, sum_ref):
    back, sums = norm_back(
        pix_ref[...].astype(F32), gain_ref[...], dot(dkv_ref[...], weight_ref[...], NT)
    )
    out_ref[...] = back.astype(BF16)

    @pl.when(pl.program_id(0) == 0)
    def _():
        sum_ref[...] = jnp.zeros_like(sum_ref)

    sum_ref[...] += sums


def pix_back(dkv, weight, pixels, gain):
    rows, width = pixels.shape
    wide = weight.shape[1]
    block = 384 if rows % 384 == 0 else 128
    return pl.pallas_call(
        pix_back_kernel,
        grid=(rows // block,),
        in_specs=[
            pl.BlockSpec((block, wide), lambda i: (i, 0)),
            pl.BlockSpec((width, wide), lambda i: (0, 0)),
            pl.BlockSpec((block, width), lambda i: (i, 0)),
            pl.BlockSpec((1, width), lambda i: (0, 0)),
        ],
        out_specs=[
            pl.BlockSpec((block, width), lambda i: (i, 0)),
            pl.BlockSpec((8, width), lambda i: (0, 0)),
        ],
        out_shape=[shape_of((rows, width), BF16), shape_of((8, width), F32)],
        compiler_params=params(),
        cost_estimate=cost(2 * rows * width * wide, 2 * rows * (2 * width + wide)),
        name="pix_back",
    )(dkv, weight, pixels, gain)


def block_index(order, **at):
    return tuple(at[label] for label in order)


def weight_half_kernel(order, sizes, number, *refs):
    lefts = refs[1 : 1 + number]
    rights = refs[1 + number : 1 + 2 * number]
    other = refs[1 + 2 * number] if len(refs) == 3 + 2 * number else None
    out_ref = refs[-1]
    begin = 0
    for left, right in zip(lefts, rights):
        grad = dot(left[...], right[...], TN)
        end = begin + grad.shape[1]
        rows = grad.shape[0] // (sizes["a"] * sizes["b"])
        for a in range(sizes["a"]):
            for b in range(sizes["b"]):
                at = block_index(order, x=0, a=a, b=b)
                spot = a * sizes["b"] + b
                part = grad[spot * rows : (spot + 1) * rows]
                if other is not None:
                    part = part + other[at + (slice(None), slice(begin, end))].astype(F32)
                out_ref[at + (slice(None), slice(begin, end))] = part.astype(BF16)
        begin = end


def weight_half(pairs, half, other, order):
    sizes = grid_sizes()
    blocks = 2 * sizes["x"]
    depth, tall = pairs[0][0].shape
    widths = [right.shape[1] // blocks for _, right in pairs]
    rows = tall // (sizes["a"] * sizes["b"])
    full = tuple(sizes[label] for label in order) + (rows, sum(widths))
    part = tuple(1 if label == "x" else sizes[label] for label in order) + (rows, sum(widths))

    def spot(i, h):
        return tuple(i if label == "x" else 0 for label in order) + (0, 0)

    out_spec = pl.BlockSpec(part, spot)
    others = [] if other is None else [other]
    moved = 2 * tall * sum(widths) * sizes["x"] * (1 + len(others))
    return pl.pallas_call(
        functools.partial(weight_half_kernel, order, sizes, len(pairs)),
        grid_spec=pltpu.PrefetchScalarGridSpec(
            num_scalar_prefetch=1,
            grid=(sizes["x"],),
            in_specs=[pl.BlockSpec((depth, tall), lambda i, h: (0, 0)) for _ in pairs]
            + [pl.BlockSpec((depth, w), lambda i, h: (0, 2 * i + h[0])) for w in widths]
            + [out_spec for _ in others],
            out_specs=out_spec,
        ),
        out_shape=shape_of(full, BF16),
        compiler_params=params(),
        cost_estimate=cost(2 * depth * tall * sum(widths) * sizes["x"], moved),
        name="weight_half",
    )(half, *[left for left, _ in pairs], *[right for _, right in pairs], *others)


def pix_weight_kernel(order, sizes, *refs):
    left_ref = refs[1]
    rights = refs[2 : 2 + sizes["x"]]
    others = refs[2 + sizes["x"] : -2]
    out_ref, total_ref = refs[-2:]
    step = pl.program_id(0)
    left = left_ref[...]
    for x in range(sizes["x"]):
        grad = dot(left, rights[x][...], TN)

        @pl.when(step == 0)
        def _():
            total_ref[x] = grad

        @pl.when(step > 0)
        def _():
            total_ref[x] += grad

    @pl.when(step == pl.num_programs(0) - 1)
    def _():
        rows = left_ref.shape[1] // (sizes["a"] * sizes["b"])
        for x in range(sizes["x"]):
            for a in range(sizes["a"]):
                for b in range(sizes["b"]):
                    at = block_index(order, x=x, a=a, b=b)
                    spot = a * sizes["b"] + b
                    part = total_ref[x, spot * rows : (spot + 1) * rows]
                    for other in others:
                        part = part + other[at].astype(F32)
                    out_ref[at] = part.astype(BF16)


def pix_weight_half(left, right, half, other, order):
    sizes = grid_sizes()
    depth, tall = left.shape
    width = right.shape[1] // (2 * sizes["x"])
    rows = tall // (sizes["a"] * sizes["b"])
    full = tuple(sizes[label] for label in order) + (rows, width)
    others = [] if other is None else [other]
    block = 768 if depth % 768 == 0 else 128
    whole = pl.BlockSpec(full, lambda i, h: (0,) * len(full))
    return pl.pallas_call(
        functools.partial(pix_weight_kernel, order, sizes),
        grid_spec=pltpu.PrefetchScalarGridSpec(
            num_scalar_prefetch=1,
            grid=(depth // block,),
            in_specs=[pl.BlockSpec((block, tall), lambda i, h: (i, 0))]
            + [
                pl.BlockSpec((block, width), lambda i, h, x=x: (i, 2 * x + h[0]))
                for x in range(sizes["x"])
            ]
            + [whole for _ in others],
            out_specs=whole,
            scratch_shapes=[pltpu.VMEM((sizes["x"], tall, width), F32)],
        ),
        out_shape=shape_of(full, BF16),
        compiler_params=params(),
        cost_estimate=cost(2 * depth * tall * width * sizes["x"], 2 * depth * (tall + width)),
        name="pix_weight_half",
    )(half, left, *[right for _ in range(sizes["x"])], *others)


def start_loads(sources, targets, sems):
    copies = [
        pltpu.make_async_copy(source, target, sems.at[i])
        for i, (source, target) in enumerate(zip(sources, targets))
    ]
    for copy in copies:
        copy.start()
    return copies


def self_softmax(query, keys):
    scores = dot(query, keys, NT) * LANES**-0.5
    expo = jnp.exp(scores - jnp.max(scores, axis=-1, keepdims=True))
    return expo / jnp.sum(expo, axis=-1, keepdims=True)


def latent_forward_kernel(
    group_rows,
    part_count,
    *refs,
):
    parts = refs[:part_count]
    (
        lat_ref,
        d_act_ref,
        self_gain_ref,
        mlp_gain_ref,
        w_cross_hbm,
        w_qkv_hbm,
        w_self_hbm,
        w_in_hbm,
        cross_ref,
        stat_ref,
        first_ref,
        self_low_ref,
        qkv_ref,
        inner_ref,
        second_ref,
        mlp_low_ref,
        act_ref,
        d_hidden_ref,
        w_cross,
        w_qkv,
        w_self,
        w_in,
        sems,
    ) = refs[part_count:]
    loads = start_loads(
        (w_cross_hbm, w_qkv_hbm, w_self_hbm, w_in_hbm), (w_cross, w_qkv, w_self, w_in), sems
    )
    rows, width = lat_ref.shape
    if part_count == 1:
        cross_ref[...] = parts[0][:, :width]
        stat_ref[...] = unpack_stat(parts[0][:, width:])
    else:
        joined = parts[0][...]
        for i, part in enumerate(parts[1:]):
            mixed, stat = merge(joined, part[...], width)
            if i < part_count - 2:
                joined = jnp.concatenate(
                    [m.astype(BF16) for m in mixed] + [pack_stat(stat).astype(BF16)], axis=1
                )
        for h in range(HEADS):
            cross_ref[:, head(h)] = mixed[h].astype(BF16)
        stat_ref[...] = stat
    loads[0].wait()
    first = lat_ref[...].astype(F32) + dot(cross_ref[...], w_cross[...])
    first_ref[...] = first
    self_low_ref[...] = norm_low(first, self_gain_ref[...])
    loads[1].wait()
    for part in range(3):
        cols = slice(part * width, (part + 1) * width)
        qkv_ref[:, cols] = dot(self_low_ref[...], w_qkv[:, cols]).astype(BF16)
    for g in range(rows // group_rows):
        at = slice(g * group_rows, (g + 1) * group_rows)
        for h in range(HEADS):
            probs = self_softmax(qkv_ref[at, head(h)], qkv_ref[at, head(h, width)])
            inner_ref[at, head(h)] = dot(
                probs.astype(BF16), qkv_ref[at, head(h, 2 * width)]
            ).astype(BF16)
    loads[2].wait()
    second = first_ref[...] + dot(inner_ref[...], w_self[...])
    second_ref[...] = second
    mlp_low_ref[...] = norm_low(second, mlp_gain_ref[...])
    loads[3].wait()
    chunk = 512

    def step(i, carry):
        cols = pl.ds(pl.multiple_of(i * chunk, chunk), chunk)
        hidden = dot(mlp_low_ref[...], w_in[:, cols])
        gate = 0.5 + 0.5 * lax.erf(hidden * 0.5**0.5)
        bell = jnp.exp(-0.5 * hidden * hidden) * 0.3989422804014327
        act_ref[:, cols] = (hidden * gate).astype(BF16)
        d_hidden_ref[:, cols] = (d_act_ref[:, cols] * (gate + hidden * bell)).astype(BF16)
        return carry

    lax.fori_loop(0, w_in.shape[1] // chunk, step, 0)


def latent_forward(parts, group_rows, latents, d_act, self_gain, mlp_gain, weights):
    rows, width = latents.shape
    hidden = d_act.shape[1]
    vmem = pl.BlockSpec(memory_space=pltpu.VMEM)
    return pl.pallas_call(
        functools.partial(latent_forward_kernel, group_rows, len(parts)),
        in_specs=[vmem] * (len(parts) + 4) + [ANY] * 4,
        out_specs=[vmem] * 10,
        out_shape=[
            shape_of((rows, width), BF16),
            shape_of((rows, LANES), F32),
            shape_of((rows, width), F32),
            shape_of((rows, width), BF16),
            shape_of((rows, 3 * width), BF16),
            shape_of((rows, width), BF16),
            shape_of((rows, width), F32),
            shape_of((rows, width), BF16),
            shape_of((rows, hidden), BF16),
            shape_of((rows, hidden), BF16),
        ],
        scratch_shapes=[pltpu.VMEM(w.shape, BF16) for w in weights]
        + [pltpu.SemaphoreType.DMA((4,))],
        compiler_params=params(),
        cost_estimate=cost(
            2 * rows * sum(w.size for w in weights),
            2 * sum(w.size for w in weights) + 4 * d_act.size,
            2 * d_act.size,
        ),
        name="latent_forward",
    )(*parts, latents, d_act, self_gain, mlp_gain, *weights)


def latent_backward_kernel(
    group_rows,
    d_hidden_ref,
    cot_ref,
    second_ref,
    first_ref,
    qkv_ref,
    cross_ref,
    stat_ref,
    self_gain_ref,
    mlp_gain_ref,
    w_in_hbm,
    w_self_hbm,
    w_qkv_hbm,
    w_cross_hbm,
    d_second_low_ref,
    d_qkv_ref,
    d_first_ref,
    d_first_low_ref,
    d_cross_ref,
    mlp_sum_ref,
    self_sum_ref,
    w_in,
    w_self,
    w_qkv,
    w_cross,
    d_inner,
    sems,
):
    loads = start_loads(
        (w_in_hbm, w_self_hbm, w_qkv_hbm, w_cross_hbm), (w_in, w_self, w_qkv, w_cross), sems
    )
    rows, width = cot_ref.shape
    scale = LANES**-0.5
    loads[0].wait()
    back, mlp_sum_ref[...] = norm_back(
        second_ref[...], mlp_gain_ref[...], dot(d_hidden_ref[...], w_in[...], NT)
    )
    d_second = cot_ref[...].astype(F32) + back
    d_first_ref[...] = d_second
    d_second_low_ref[...] = d_second.astype(BF16)
    loads[1].wait()
    d_inner[...] = dot(d_second_low_ref[...], w_self[...], NT).astype(BF16)
    for g in range(rows // group_rows):
        at = slice(g * group_rows, (g + 1) * group_rows)
        for h in range(HEADS):
            query = qkv_ref[at, head(h)]
            keys = qkv_ref[at, head(h, width)]
            grad = d_inner[at, head(h)]
            probs = self_softmax(query, keys)
            d_probs = dot(grad, qkv_ref[at, head(h, 2 * width)], NT)
            along = jnp.sum(probs * d_probs, axis=-1, keepdims=True)
            d_scores = (probs * (d_probs - along)).astype(BF16)
            d_qkv_ref[at, head(h)] = (dot(d_scores, keys) * scale).astype(BF16)
            d_qkv_ref[at, head(h, width)] = (dot(d_scores, query, TN) * scale).astype(BF16)
            d_qkv_ref[at, head(h, 2 * width)] = dot(probs.astype(BF16), grad, TN).astype(BF16)
    loads[2].wait()
    back, self_sum_ref[...] = norm_back(
        first_ref[...], self_gain_ref[...], dot(d_qkv_ref[...], w_qkv[...], NT)
    )
    d_first = d_first_ref[...] + back
    d_first_ref[...] = d_first
    d_first_low_ref[...] = d_first.astype(BF16)
    loads[3].wait()
    d_cross = dot(d_first_low_ref[...], w_cross[...], NT).astype(BF16)
    d_cross_ref[:, :width] = d_cross
    lane = lax.broadcasted_iota(jnp.int32, (rows, LANES), 1)
    delta = jnp.zeros((rows, LANES), F32)
    for h in range(HEADS):
        along = d_cross[:, head(h)].astype(F32) * cross_ref[:, head(h)].astype(F32)
        delta = jnp.where(lane == h, jnp.sum(along, axis=-1, keepdims=True), delta)
    packed = pack_stat(stat_ref[...]) + pltpu.roll(pack_stat(delta), 3 * HEADS, 1)
    d_cross_ref[:, width:] = packed.astype(BF16)


def latent_backward(group_rows, arrays, weights):
    d_hidden, cot = arrays[:2]
    rows, width = cot.shape
    vmem = pl.BlockSpec(memory_space=pltpu.VMEM)
    return pl.pallas_call(
        functools.partial(latent_backward_kernel, group_rows),
        in_specs=[vmem] * len(arrays) + [ANY] * 4,
        out_specs=[vmem] * 7,
        out_shape=[
            shape_of((rows, width), BF16),
            shape_of((rows, 3 * width), BF16),
            shape_of((rows, width), F32),
            shape_of((rows, width), BF16),
            shape_of((rows, width + LANES), BF16),
            shape_of((8, width), F32),
            shape_of((8, width), F32),
        ],
        scratch_shapes=[pltpu.VMEM(w.shape, BF16) for w in weights]
        + [pltpu.VMEM((rows, width), BF16), pltpu.SemaphoreType.DMA((4,))],
        compiler_params=params(),
        cost_estimate=cost(
            2 * rows * sum(w.size for w in weights), 2 * sum(w.size for w in weights)
        ),
        name="latent_backward",
    )(*arrays, *weights)


def reduced_weights(pairs, order):
    core = lax.rem(lax.axis_index("pix"), 2).astype(jnp.int32)
    sent = weight_half(pairs, jnp.reshape(1 - core, (1,)), None, order)
    kept = weight_half(pairs, jnp.reshape(core, (1,)), from_core(sent), order)
    total = reduce_parts(kept, order)
    begin, out = 0, []
    for _, right in pairs:
        width = right.shape[1] // lax.axis_size("pix")
        out.append(total[:, begin : begin + width])
        begin += width
    return out


def reduced_pix_weight(left, right, order):
    core = lax.rem(lax.axis_index("pix"), 2).astype(jnp.int32)
    sent = pix_weight_half(left, right, jnp.reshape(1 - core, (1,)), None, order)
    kept = pix_weight_half(left, right, jnp.reshape(core, (1,)), from_core(sent), order)
    return reduce_parts(kept, order)


def shards(
    latents,
    pixels,
    pixel_mask,
    cotangent,
    lat_gain,
    pix_gain,
    self_gain,
    mlp_gain,
    w_query,
    w_kv,
    w_cross_out,
    w_qkv,
    w_self_out,
    w_mlp_in,
    w_mlp_out,
):
    sizes = grid_sizes()
    own, group_rows, width = latents.shape
    groups, slots = pixel_mask.shape
    rows = own * group_rows
    lat_rows = latents.reshape(rows, width)
    cot_rows = cotangent.reshape(rows, width)
    pix_rows = pixels.reshape(groups * slots, width)
    gain_rows = [g.reshape(1, width) for g in (lat_gain, pix_gain, self_gain, mlp_gain)]
    lat_gain, pix_gain, self_gain, mlp_gain = gain_rows
    counts = jnp.sum(pixel_mask, axis=1, dtype=jnp.int32)

    here = lax.axis_index("pix")
    here_x, here_c = here // 2, lax.rem(here, 2)

    def groups_of(turn):
        holder_x = lax.rem(here_x + turn, sizes["x"])
        holders = [holder_x * 2 + here_c, holder_x * 2 + 1 - here_c]
        return [holder * own + i for holder in holders for i in range(own)]

    near = jnp.stack(groups_of(0)).astype(jnp.int32)
    turns = range(1, sizes["x"])
    far = [g for turn in turns for g in groups_of(turn)]
    far = jnp.stack(far).astype(jnp.int32) if far else None

    def spread(value):
        fars = []
        for turn in turns:
            moved = from_x(value, turn)
            fars += [moved, from_core(moved)]
        return jnp.concatenate([value, from_core(value)]), jnp.concatenate(fars)

    lat_low = norm_low(lat_rows.astype(F32), lat_gain)
    query = dot(lat_low, w_query).astype(BF16).reshape(own, group_rows, width)
    query_near, query_far = spread(query)
    pix_low, kv_rows = pix_project(pix_rows, pix_gain, w_kv)
    kv = kv_rows.reshape(groups, slots, 2 * width)

    mixed_far = cross_forward(far, counts, query_far, kv)
    mixed_far = mixed_far.reshape(sizes["x"] - 1, 2, own, group_rows, width + LANES)
    parts = []
    for turn in turns:
        joined = merge_call(mixed_far[turn - 1, 0], from_core(mixed_far[turn - 1, 1]))
        parts.append(from_x(joined, sizes["x"] - turn).reshape(rows, width + LANES))
    mixed_near = cross_forward(near, counts, query_near, kv)
    mixed_near = mixed_near.reshape(2, own, group_rows, width + LANES)
    joined = merge_call(mixed_near[0], from_core(mixed_near[1]))
    parts = [joined.reshape(rows, width + LANES)] + parts

    d_act = dot(cot_rows, w_mlp_out, NT)
    (
        cross_low,
        cross_stat,
        first,
        self_low,
        qkv,
        inner_low,
        second,
        mlp_low,
        act,
        d_hidden,
    ) = latent_forward(
        parts,
        group_rows,
        lat_rows,
        d_act,
        self_gain,
        mlp_gain,
        (w_cross_out, w_qkv, w_self_out, w_mlp_in),
    )
    latents_out = (second + dot(act, w_mlp_out)).astype(BF16)
    (sum_out,) = reduced_weights([(act, cot_rows)], "bxa")
    (sum_in,) = reduced_weights([(mlp_low, d_hidden)], "axb")
    d_second_low, d_qkv, d_first, d_first_low, d_cross, mlp_sum, self_sum = latent_backward(
        group_rows,
        (
            d_hidden,
            cot_rows,
            second,
            first,
            qkv,
            cross_low,
            cross_stat,
            self_gain,
            mlp_gain,
        ),
        (w_mlp_in, w_self_out, w_qkv, w_cross_out),
    )
    cross_near, cross_far = spread(d_cross.reshape(own, group_rows, width + LANES))
    sum_self, sum_qkv, sum_cross = reduced_weights(
        [(inner_low, d_second_low), (self_low, d_qkv), (cross_low, d_first_low)], "xba"
    )
    dq_near, d_kv = cross_backward(near, counts, query_near, cross_near, kv, None)
    dq_far, d_kv = cross_backward(far, counts, query_far, cross_far, kv, d_kv)
    dq_far = dq_far.reshape(sizes["x"] - 1, 2, own, group_rows, width)
    dq_near = dq_near.reshape(2, own, group_rows, width)
    terms = [dq_near[0], from_core(dq_near[1])]
    for turn in turns:
        joined = add_low(dq_far[turn - 1, 0], from_core(dq_far[turn - 1, 1]))
        terms.append(from_x(joined, sizes["x"] - turn))
    d_query = add_low(*terms).reshape(rows, width)
    d_kv_rows = d_kv.reshape(groups * slots, 2 * width)
    sum_kv = reduced_pix_weight(pix_low, d_kv_rows, "bxa")
    d_pixels, pix_sum = pix_back(d_kv_rows, w_kv, pix_rows, pix_gain)
    (sum_query,) = reduced_weights([(lat_low, d_query)], "xba")
    back, lat_sum = norm_back(lat_rows.astype(F32), lat_gain, dot(d_query, w_query, NT))
    d_latents = d_first + back
    gain_sums = jnp.stack([s.sum(0) for s in (lat_sum, pix_sum, self_sum, mlp_sum)])
    gain_sums = reduce_gains(gain_sums)
    return (
        latents_out.reshape(latents.shape),
        d_latents.reshape(latents.shape),
        d_pixels.reshape(pixels.shape),
        gain_sums[0],
        gain_sums[1],
        gain_sums[2],
        gain_sums[3],
        sum_query,
        sum_kv,
        sum_cross,
        sum_qkv,
        sum_self,
        sum_in,
        sum_out,
    )


def solution(mesh):
    held = P(("dp", "pix"), None, None)
    return jax.shard_map(
        shards,
        mesh=mesh,
        in_specs=(held, P("dp", "pix", None), P("dp", "pix"), held) + (P(),) * 11,
        out_specs=(held, held, P("dp", "pix", None)) + (P("dp"),) * 4 + (P("dp", "pix"),) * 7,
        check_vma=False,
    )
```

time: 1230 us -> 522 us (0.42)
  waiting for transfers between devices: 803 us -> 107 us
  Pallas kernels: 0 us -> 219 us
  matrix products: 206 us -> 17.9 us
  starting transfers between devices: 1.31 us -> 124 us
  blocking collectives: 50.2 us -> 0 us
  other arithmetic: 73.8 us -> 26.8 us
  local copies, waits for them, and re-layouts: 68.6 us -> 21.7 us
  between operations: 15.8 us -> 1.94 us
    reduce_scatter x16 -> x0, waiting for transfers between devices: 780 us -> none  [the longest x1 144 us: shards(): lax.psum_scatter(d_w_mlp_in.astype(jnp.bfloat16), 'dp', scatter_dimension...]
    pallas_call x0 -> x20, Pallas kernels: none -> 219 us  [the longest x8 36.1 us: weight_half(): pl.pallas_call(functools.partial(weight_half_kernel, order, sizes, len(pa...]
    dot_general x32 -> x4, matrix products: 204 us -> 17.9 us  [dot(): return lax.dot_general(left, right, dims, preferred_element_type=F32)]
    ppermute x0 -> x66, starting transfers between devices: none -> 124 us  [move(): return lax.ppermute(value, axis, pairs)]
    ppermute x0 -> x66, waiting for transfers between devices: none -> 107 us  [move(): return lax.ppermute(value, axis, pairs)]
    reshape x9 -> x0, local copies, waits for them, and re-layouts: 34.8 us -> none  [the longest x5 20.8 us: join_heads(): tensor_in.reshape(tensor_in.shape[0], tensor_in.shape[1], tensor_in.shape...]
    convert_element_type x19 -> x33, other arithmetic: 45.6 us -> 14.5 us  [the longest x27 9.82 us: add_low(): return total.astype(terms[0].dtype)]
    all_gather x2 -> x0, waiting for transfers between devices: 22.7 us -> none  [the longest x1 22.7 us: shards(): d_cross_all = lax.all_gather(d_cross, 'pix', axis=0, tiled=True)]
  transfers between devices with their start and end apart: 18 -> 66, of which waited for: 15 -> 14; matrix products, arithmetic and copies ran while one was open for 16% -> 9% of each run, Pallas kernels for 0% -> 29%
where the time goes in v1:
time: 522 us; the launch traced here: 518 us
  Pallas kernels  219 us (42%)
  starting transfers between devices  124 us (24%)
  waiting for transfers between devices  107 us (20%)
  other arithmetic  26.8 us (5%)
  local copies, waits for them, and re-layouts  21.7 us (4%)
  matrix products  17.9 us (3%)
    ppermute x66, starting transfers between devices, move(): return lax.ppermute(value, axis, pairs)  124 us
    ppermute x66, waiting for transfers between devices, move(): return lax.ppermute(value, axis, pairs)  107 us
    pallas_call x8, Pallas kernels, weight_half(): pl.pallas_call(functools.partial(weight_half_kernel, order, sizes, len(pa...  36.1 us
    pallas_call x2, Pallas kernels, pix_weight_half(): pl.pallas_call(functools.partial(pix_weight_kernel, order, sizes), grid_s...  26.8 us
    pallas_call x2, Pallas kernels, cross_backward(): pl.pallas_call(cross_backward_kernel, grid_spec=pltpu.PrefetchScalarGridS...  26.2 us
    pallas_call x2, Pallas kernels, cross_forward(): pl.pallas_call(cross_forward_kernel, grid_spec=pltpu.PrefetchScalarGridSp...  24.3 us
    pallas_call x1, Pallas kernels, pix_back(): pl.pallas_call(pix_back_kernel, grid=(rows // block,), in_specs=[pl.Block...  23.3 us
    pallas_call x1, Pallas kernels, latent_forward(): pl.pallas_call(functools.partial(latent_forward_kernel, group_rows, len(p...  22 us
  transfers between devices with their start and end apart: 66, of which 14 were waited for; matrix products, arithmetic and copies ran while one was open for 9% of the time, Pallas kernels for 29%

profile of v1, /device:TPU:0, one launch (start us, length us, event | category | flops | bytes accessed | tf_op | source)
XLA Modules:
  0.0 517.9 jit_solution(13991149308792100615)
XLA Ops:
  9.2 12.1 %collective-permute-done.2 = bf16[2,128,1024]{2,1,0:T(8,128)(2,1)S(1)} collective-permute-done((bf16[2,128,1024]{2,1,0:T(8,128)(2,1)}, bf16[2,128,1024]{2,1,0:T(8,128)(2,1)S(1)}, u32[]{:S(2)}, u32[]{:S(2)}) %collective-permute-start.2) | collective-permute-done | bytes 524320 | tf_op jit(solution)/shard_map/ppermute | solution.py:49
  21.3 21.2 %pix_project.1 = (bf16[3072,1024]{1,0:T(8,128)(2,1)}, bf16[3072,2048]{1,0:T(8,128)(2,1)}) custom-call(bf16[3072,1024]{1,0:T(8,128)(2,1)} %bitcast.272, f32[1,1024]{1,0:T(1,128)} %bitcast.274, bf16[1024,2048]{1,0:T(8,128)(2,1)} %weight_ref.3), custom_call_target="tpu_custom_call" | custom-call | flops 12884901888 | bytes 25165824 | tf_op jit(solution)/shard_map/pix_project/pallas_call | solution.py:195
  48.8 12.1 %cross_forward.3 = bf16[4,128,1152]{2,1,0:T(8,128)(2,1)} custom-call(s32[4]{0:T(128)} %pad_add_fusion.1.group_ref, s32[8]{0:T(128)} %reduce_sum.78.count_ref.old_ref, bf16[4,128,1024]{2,1,0:T(8,128)(2,1)} %copy-done.7, bf16[8,384,2048]{2,1,0:T(8,128)(2,1)} %bitcast.232), custom_call_target="tpu_custom_call" | custom-call | flops 1610612736 | bytes 6291456 | tf_op jit(solution)/shard_map/cross_forward/pallas_call | solution.py:238
  63.6 12.1 %cross_forward.2 = bf16[4,128,1152]{2,1,0:T(8,128)(2,1)} custom-call(s32[4]{0:T(128)} %pad_add_fusion.group_ref, s32[8]{0:T(128)} %reduce_sum.78.count_ref.old_ref, bf16[4,128,1024]{2,1,0:T(8,128)(2,1)} %pad_maximum_fusion.2.query_ref, bf16[8,384,2048]{2,1,0:T(8,128)(2,1)} %bitcast.233), custom_call_target="tpu_custom_call" | custom-call | flops 1610612736 | bytes 6291456 | tf_op jit(solution)/shard_map/cross_forward/pallas_call | solution.py:238
  83.3 7.8 %fusion.52.refs_3_ = f32[256,4096]{1,0:T(8,128)} fusion(bf16[256,1024]{1,0:T(8,128)(2,1)S(1)} %bitcast.243, bf16[4096,1024]{1,0:T(8,128)(2,1)} %param.29), kind=kOutput, calls=%fused_computation.149 | convolution fusion | flops 2147483648 | bytes 13107200 | tf_op jit(solution)/shard_map/dot_general | solution.py:113
  91.9 14.4 %merge.2 = bf16[2,128,1152]{2,1,0:T(8,128)(2,1)} custom-call(bf16[2,128,1152]{2,1,0:T(8,128)(2,1)} %get-tuple-element.78.first_ref, bf16[2,128,1152]{2,1,0:T(8,128)(2,1)} %copy-done.16), custom_call_target="tpu_custom_call" | custom-call | flops 2359296 | bytes 1769472 | tf_op jit(solution)/shard_map/merge/pallas_call | solution.py:269
  107.1 22.0 %latent_forward.1 = (bf16[256,1024]{1,0:T(8,128)(2,1)}, f32[256,128]{1,0:T(8,128)}, f32[256,1024]{1,0:T(8,128)}, bf16[256,1024]{1,0:T(8,128)(2,1)}, bf16[256,307...) custom-call(bf16[256,1152]{1,0:T(8,128)(2,1)} %bitcast.247, ...), custom_call_target="tpu_custom_call" | custom-call | flops 4831838208 | bytes 23068672 | tf_op jit(solution)/shard_map/latent_forward/pallas_call | solution.py:594
  129.1 21.6 %latent_backward.1 = (bf16[256,1024]{1,0:T(8,128)(2,1)}, bf16[256,3072]{1,0:T(8,128)(2,1)}, f32[256,1024]{1,0:T(8,128)}, bf16[256,1024]{1,0:T(8,128)(2,1)}, bf16...) custom-call(bf16[256,4096]{1,0:T(8,128)(2,1)} %get-tuple-element.42.d_hidden_ref.refs_2_, ...), custom_call_target="tpu_custom_call" | custom-call | flops 4831838208 | bytes 18874368 | tf_op jit(solution)/shard_map/latent_backward/pallas_call | solution.py:701
  151.0 15.4 %collective-permute-done.8 = bf16[2,128,1152]{2,1,0:T(8,128)(2,1)S(1)} collective-permute-done((bf16[2,128,1152]{2,1,0:T(8,128)(2,1)}, bf16[2,128,1152]{2,1,0:T(8,128)(2,1)S(1)}, u32[]{:S(2)}, u32[]{:S(2)}) %collective-permute-start.8) | collective-permute-done | bytes 589856 | tf_op jit(solution)/shard_map/ppermute | solution.py:49
  168.6 12.9 %cross_backward.2 = (bf16[4,128,1024]{2,1,0:T(8,128)(2,1)}, bf16[8,384,2048]{2,1,0:T(8,128)(2,1)}) custom-call(s32[4]{0:T(128)} %pad_add_fusion.group_ref, s32[8]{0:T(128)} %reduce_sum.78.count_ref.old_ref, bf16[4,128,1024]{2,1,0:T(8,128)(2,1)} %pad_maximum_fusion.2.query_ref, bf16[4,128,1152]{2,1,0:T(8,128)(2,1)} %pad_maximum_fusion.grad_ref, ...), custom_call_target="tpu_custom_call" | custom-call | flops 2013265920 | bytes 12582912 | tf_op jit(solution)/shard_map/cross_backward/pallas_call | solution.py:309
  182.7 13.3 %cross_backward.3 = (bf16[4,128,1024]{2,1,0:T(8,128)(2,1)}, bf16[8,384,2048]{2,1,0:T(8,128)(2,1)}) custom-call(s32[4]{0:T(128)} %pad_add_fusion.1.group_ref, s32[8]{0:T(128)} %reduce_sum.78.count_ref.old_ref, bf16[4,128,1024]{2,1,0:T(8,128)(2,1)} %copy-done.7, bf16[4,128,1152]{2,1,0:T(8,128)(2,1)} %pad_maximum_fusion.1.grad_ref, ...), custom_call_target="tpu_custom_call", output_to_operand_aliasing={{1}: (5, {})} | custom-call | flops 2013265920 | bytes 12582912 | tf_op jit(solution)/shard_map/cross_backward/pallas_call | solution.py:309
  202.7 23.3 %pix_back.1 = (bf16[3072,1024]{1,0:T(8,128)(2,1)}, f32[8,1024]{1,0:T(8,128)}) custom-call(bf16[3072,2048]{1,0:T(8,128)(2,1)} %bitcast.227, bf16[1024,2048]{1,0:T(8,128)(2,1)} %weight_ref.3, bf16[3072,1024]{1,0:T(8,128)(2,1)} %bitcast.273, f32[1,1024]{1,0:T(1,128)} %bitcast.275), custom_call_target="tpu_custom_call" | custom-call | flops 12884901888 | bytes 25165824 | tf_op jit(solution)/shard_map/pix_back/pallas_call | solution.py:352
  240.6 4.7 weight_half.14
  248.4 5.1 weight_half.10
  254.8 5.2 %collective-permute-start.15 = (f32[4,128]{1,0:T(4,128)S(1)}, f32[4,128]{1,0:T(4,128)S(1)}, u32[]{:S(2)}, u32[]{:S(2)}) collective-permute-start(f32[4,128]{1,0:T(4,128)S(1)} %add.344), channel_id=1, source_target_pairs={{0,8},{8,16},{16,24},{4,12},{12,20},{20,28},{1,9},{9,17},{17,25},{... | collective-permute-start | bytes 6152 | tf_op jit(solution)/shard_map/ppermute | solution.py:49
  263.6 12.9 %pix_weight_half.2 = bf16[2,2,4,128,512]{4,3,2,1,0:T(8,128)(2,1)} custom-call(s32[1]{0:T(128)} %bitcast.52.refs_0_, bf16[3072,1024]{1,0:T(8,128)(2,1)} %get-tuple-element.57.refs_1_, bf16[3072,2048]{1,0:T(8,128)(2,1)} %bitcast.228, bf16[3072,2048]{1,0:T(8,128)(2,1)} %bitcast.229), custom_call_target="tpu_custom_call" | custom-call | flops 6442450944 | bytes 9437184 | tf_op jit(solution)/shard_map/pix_weight_half/pallas_call | solution.py:470
  276.7 6.7 %fusion.11 = bf16[256,1024]{1,0:T(8,128)(2,1)} fusion(f32[256,1024]{1,0:T(8,128)} %get-tuple-element.40.second_ref, bf16[256,4096]{1,0:T(8,128)(2,1)S(1)} %copy-done.6, bf16[4096,1024]{1,0:T(8,128)(2,1)} %param.29), kind=kOutput, calls=%fused_computation.27 | convolution fusion | flops 2148007936 | bytes 12058624 | tf_op jit(solution)/shard_map/dot_general | solution.py:113
  291.0 11.9 %collective-permute-done.22 = bf16[2,4,128,256]{3,2,1,0:T(8,128)(2,1)S(1)} collective-permute-done((bf16[2,4,128,256]{3,2,1,0:T(8,128)(2,1)S(1)}, bf16[2,4,128,256]{3,2,1,0:T(8,128)(2,1)S(1)}, u32[]{:S(2)}, u32[]{:S(2)}) %collective-permute-start.22) | collective-permute-done | bytes 524320 | tf_op jit(solution)/shard_map/ppermute | solution.py:49
  303.7 13.9 %pix_weight_half.3 = bf16[2,2,4,128,512]{4,3,2,1,0:T(8,128)(2,1)} custom-call(s32[1]{0:T(128)} %bitcast.51.refs_0_, bf16[3072,1024]{1,0:T(8,128)(2,1)} %get-tuple-element.57.refs_1_, bf16[3072,2048]{1,0:T(8,128)(2,1)} %bitcast.230, bf16[3072,2048]{1,0:T(8,128)(2,1)} %bitcast.231, bf16[2,2,4,128,512]{4,3,2,1,0:T(8,128)(2,1)} %collective-permute-done.30.refs_4_), custom_call_target="tpu_custom_call" | custom-call | flops 6442450944 | bytes 9437184 | tf_op jit(solution)/shard_map/pix_weight_half/pallas_call | solution.py:470
  331.3 4.8 weight_half.13
  340.0 5.5 %weight_half.15 = bf16[2,2,4,512,256]{4,3,2,1,0:T(8,128)(2,1)} custom-call(s32[1]{0:T(128)} %bitcast.51.refs_0_, bf16[256,4096]{1,0:T(8,128)(2,1)} %get-tuple-element.41.refs_1_, bf16[256,1024]{1,0:T(8,128)(2,1)} %bitcast.242, bf16[2,2,4,512,256]{4,3,2,1,0:T(8,128)(2,1)} %collective-permute-done.57.refs_3_), custom_call_target="tpu_custom_call" | custom-call | flops 1073741824 | bytes 8388608 | tf_op jit(solution)/shard_map/weight_half/pallas_call | solution.py:412
  346.6 5.9 %weight_half.11 = bf16[2,2,4,128,1280]{4,3,2,1,0:T(8,128)(2,1)} custom-call(s32[1]{0:T(128)} %bitcast.51.refs_0_, bf16[256,1024]{1,0:T(8,128)(2,1)} %get-tuple-element.58.refs_1_, bf16[256,1024]{1,0:T(8,128)(2,1)} %get-tuple-element.59.refs_2_, bf16[256,1024]{1,0:T(8,128)(2,1)} %get-tuple-element.45.cross_ref.refs_3_, ...), custom_call_target="tpu_custom_call" | custom-call | flops 1342177280 | bytes 10485760 | tf_op jit(solution)/shard_map/weight_half/pallas_call | solution.py:412
  367.3 4.4 collective-permute-start.50
  373.7 19.5 %collective-permute-done.34 = bf16[128,512]{1,0:T(8,128)(2,1)S(1)} collective-permute-done((bf16[128,512]{1,0:T(8,128)(2,1)S(1)}, bf16[128,512]{1,0:T(8,128)(2,1)S(1)}, u32[]{:S(2)}, u32[]{:S(2)}) %collective-permute-start.34) | collective-permute-done | bytes 131104 | tf_op jit(solution)/shard_map/ppermute | solution.py:49
  394.7 16.5 %collective-permute-start.26 = (bf16[128,256]{1,0:T(8,128)(2,1)S(1)}, bf16[128,256]{1,0:T(8,128)(2,1)S(1)}, u32[]{:S(2)}, u32[]{:S(2)}) collective-permute-start(bf16[128,256]{1,0:T(8,128)(2,1)S(1)} %get-tuple-element.89), channel_id=1, source_target_pairs={{0,8},{8,16},{16,24},{4,12},{12,20},{20,28},{1,9},{9,17},{17,25},{... | collective-permute-start | bytes 196616 | tf_op jit(solution)/shard_map/ppermute | solution.py:49
  412.6 4.6 collective-permute-start.35
  428.9 16.0 %collective-permute-start.51 = (bf16[2,2,128,1024]{3,2,1,0:T(8,128)(2,1)S(1)}, bf16[2,2,128,1024]{3,2,1,0:T(8,128)(2,1)S(1)}, u32[]{:S(2)}, u32[]{:S(2)}) collective-permute-start(bf16[2,2,128,1024]{3,2,1,0:T(8,128)(2,1)S(1)} %get-tuple-element.67), channel_id=1, source_target_pairs={{0,8},{8,16},{16,24},{4,12},{12,20},{20,28},{1,9},{9,17},{17,25},{... | collective-permute-start | bytes 3145736 | tf_op jit(solution)/shard_map/ppermute | solution.py:49
  449.8 19.5 %collective-permute-done.60 = bf16[512,256]{1,0:T(8,128)(2,1)S(1)} collective-permute-done((bf16[512,256]{1,0:T(8,128)(2,1)S(1)}, bf16[512,256]{1,0:T(8,128)(2,1)S(1)}, u32[]{:S(2)}, u32[]{:S(2)}) %collective-permute-start.60) | collective-permute-done | bytes 262176 | tf_op jit(solution)/shard_map/ppermute | solution.py:49
  469.3 4.4 collective-permute-start.61
  479.1 4.4 collective-permute-start.62
  491.7 5.8 %collective-permute-done.43 = bf16[128,1280]{1,0:T(8,128)(2,1)S(1)} collective-permute-done((bf16[128,1280]{1,0:T(8,128)(2,1)S(1)}, bf16[128,1280]{1,0:T(8,128)(2,1)S(1)}, u32[]{:S(2)}, u32[]{:S(2)}) %collective-permute-start.43) | collective-permute-done | bytes 327712 | tf_op jit(solution)/shard_map/ppermute | solution.py:49
  508.3 7.9 %collective-permute-done.47 = bf16[128,1280]{1,0:T(8,128)(2,1)S(1)} collective-permute-done((bf16[128,1280]{1,0:T(8,128)(2,1)S(1)}, bf16[128,1280]{1,0:T(8,128)(2,1)S(1)}, u32[]{:S(2)}, u32[]{:S(2)}) %collective-permute-start.47) | collective-permute-done | bytes 327712 | tf_op jit(solution)/shard_map/ppermute | solution.py:49
  (256 shorter events, 148.4 us)
Async XLA Ops:
  9.2 35.2 %collective-permute-start = (bf16[2,128,1024]{2,1,0:T(8,128)(2,1)}, bf16[2,128,1024]{2,1,0:T(8,128)(2,1)}, u32[]{:S(2)}, u32[]{:S(2)}) collective-permute-start(bf16[2,128,1024]{2,1,0:T(8,128)(2,1)} %bitcast.7), channel_id=1, source_target_pairs={{0,1},{1,0},{2,3},{3,2},{4,5},{5,4},{6,7},{7,6},{8,9},{9,8},{10,11... | collective-permute-start | bytes 1572872 | tf_op jit(solution)/shard_map/ppermute | solution.py:49
  21.3 25.4 %collective-permute-start.3 = (bf16[2,128,1024]{2,1,0:T(8,128)(2,1)S(1)}, bf16[2,128,1024]{2,1,0:T(8,128)(2,1)}, u32[]{:S(2)}, u32[]{:S(2)}) collective-permute-start(bf16[2,128,1024]{2,1,0:T(8,128)(2,1)S(1)} %collective-permute-done.2), channel_id=1, source_target_pairs={{0,1},{1,0},{2,3},{3,2},{4,5},{5,4},{6,7},{7,6},{8,9},{9,8},{10,11... | collective-permute-start | bytes 1572872 | tf_op jit(solution)/shard_map/ppermute | solution.py:49
  81.5 24.7 %collective-permute-start.5 = (bf16[2,128,1152]{2,1,0:T(8,128)(2,1)}, bf16[2,128,1152]{2,1,0:T(8,128)(2,1)S(1)}, u32[]{:S(2)}, u32[]{:S(2)}) collective-permute-start(bf16[2,128,1152]{2,1,0:T(8,128)(2,1)} %merge.3), channel_id=1, source_target_pairs={{2,0},{0,2},{3,1},{1,3},{6,4},{4,6},{7,5},{5,7},{10,8},{8,10},{11,... | collective-permute-start | bytes 1769480 | tf_op jit(solution)/shard_map/ppermute | solution.py:49
  150.6 15.7 %collective-permute-start.8 = (bf16[2,128,1152]{2,1,0:T(8,128)(2,1)}, bf16[2,128,1152]{2,1,0:T(8,128)(2,1)S(1)}, u32[]{:S(2)}, u32[]{:S(2)}) collective-permute-start(bf16[2,128,1152]{2,1,0:T(8,128)(2,1)} %bitcast.252), channel_id=1, source_target_pairs={{2,0},{0,2},{3,1},{1,3},{6,4},{4,6},{7,5},{5,7},{10,8},{8,10},{11,... | collective-permute-start | bytes 1769480 | tf_op jit(solution)/shard_map/ppermute | solution.py:49
  151.0 15.4 %collective-permute-start.6 = (bf16[2,128,1152]{2,1,0:T(8,128)(2,1)}, bf16[2,128,1152]{2,1,0:T(8,128)(2,1)S(1)}, u32[]{:S(2)}, u32[]{:S(2)}) collective-permute-start(bf16[2,128,1152]{2,1,0:T(8,128)(2,1)} %bitcast.253), channel_id=1, source_target_pairs={{0,1},{1,0},{2,3},{3,2},{4,5},{5,4},{6,7},{7,6},{8,9},{9,8},{10,11... | collective-permute-start | bytes 1769480 | tf_op jit(solution)/shard_map/ppermute | solution.py:49
  166.4 15.2 %collective-permute-start.9 = (bf16[2,128,1152]{2,1,0:T(8,128)(2,1)S(1)}, bf16[2,128,1152]{2,1,0:T(8,128)(2,1)S(1)}, u32[]{:S(2)}, u32[]{:S(2)}) collective-permute-start(bf16[2,128,1152]{2,1,0:T(8,128)(2,1)S(1)} %collective-permute-done.8), channel_id=1, source_target_pairs={{0,1},{1,0},{2,3},{3,2},{4,5},{5,4},{6,7},{7,6},{8,9},{9,8},{10,11... | collective-permute-start | bytes 1769480 | tf_op jit(solution)/shard_map/ppermute | solution.py:49
  200.3 26.6 %collective-permute-start.7 = (bf16[2,128,1024]{2,1,0:T(8,128)(2,1)}, bf16[2,128,1024]{2,1,0:T(8,128)(2,1)}, u32[]{:S(2)}, u32[]{:S(2)}) collective-permute-start(bf16[2,128,1024]{2,1,0:T(8,128)(2,1)} %slice.54), channel_id=1, source_target_pairs={{0,1},{1,0},{2,3},{3,2},{4,5},{5,4},{6,7},{7,6},{8,9},{9,8},{10,11... | collective-permute-start | bytes 1572872 | tf_op jit(solution)/shard_map/ppermute | solution.py:49
  202.4 24.5 %collective-permute-start.11 = (bf16[2,128,1024]{2,1,0:T(8,128)(2,1)}, bf16[2,128,1024]{2,1,0:T(8,128)(2,1)}, u32[]{:S(2)}, u32[]{:S(2)}) collective-permute-start(bf16[2,128,1024]{2,1,0:T(8,128)(2,1)} %fusion.17), channel_id=1, source_target_pairs={{2,0},{0,2},{3,1},{1,3},{6,4},{4,6},{7,5},{5,7},{10,8},{8,10},{11,... | collective-permute-start | bytes 1572872 | tf_op jit(solution)/shard_map/ppermute | solution.py:49
  245.3 92.6 %collective-permute-start.57 = (bf16[2,2,4,512,256]{4,3,2,1,0:T(8,128)(2,1)}, bf16[2,2,4,512,256]{4,3,2,1,0:T(8,128)(2,1)}, u32[]{:S(2)}, u32[]{:S(2)}) collective-permute-start(bf16[2,2,4,512,256]{4,3,2,1,0:T(8,128)(2,1)} %weight_half.14), channel_id=1, source_target_pairs={{0,1},{1,0},{2,3},{3,2},{4,5},{5,4},{6,7},{7,6},{8,9},{9,8},{10,11... | collective-permute-start | bytes 12582920 | tf_op jit(solution)/shard_map/ppermute | solution.py:49
  245.3 81.8 %collective-permute-start.48 = (bf16[4,2,2,128,1024]{4,3,2,1,0:T(8,128)(2,1)}, bf16[4,2,2,128,1024]{4,3,2,1,0:T(8,128)(2,1)}, u32[]{:S(2)}, u32[]{:S(2)}) collective-permute-start(bf16[4,2,2,128,1024]{4,3,2,1,0:T(8,128)(2,1)} %weight_half.12), channel_id=1, source_target_pairs={{0,1},{1,0},{2,3},{3,2},{4,5},{5,4},{6,7},{7,6},{8,9},{9,8},{10,11... | collective-permute-start | bytes 12582920 | tf_op jit(solution)/shard_map/ppermute | solution.py:49
  253.5 93.1 %collective-permute-start.39 = (bf16[2,2,4,128,1280]{4,3,2,1,0:T(8,128)(2,1)}, bf16[2,2,4,128,1280]{4,3,2,1,0:T(8,128)(2,1)}, u32[]{:S(2)}, u32[]{:S(2)}) collective-permute-start(bf16[2,2,4,128,1280]{4,3,2,1,0:T(8,128)(2,1)} %weight_half.10), channel_id=1, source_target_pairs={{0,1},{1,0},{2,3},{3,2},{4,5},{5,4},{6,7},{7,6},{8,9},{9,8},{10,11... | collective-permute-start | bytes 15728648 | tf_op jit(solution)/shard_map/ppermute | solution.py:49
  263.1 20.4 %collective-permute-start.21 = (bf16[2,2,4,128,256]{4,3,2,1,0:T(8,128)(2,1)}, bf16[2,2,4,128,256]{4,3,2,1,0:T(8,128)(2,1)}, u32[]{:S(2)}, u32[]{:S(2)}) collective-permute-start(bf16[2,2,4,128,256]{4,3,2,1,0:T(8,128)(2,1)} %weight_half.8), channel_id=1, source_target_pairs={{0,1},{1,0},{2,3},{3,2},{4,5},{5,4},{6,7},{7,6},{8,9},{9,8},{10,11... | collective-permute-start | bytes 3145736 | tf_op jit(solution)/shard_map/ppermute | solution.py:49
  276.5 27.1 %collective-permute-start.30 = (bf16[2,2,4,128,512]{4,3,2,1,0:T(8,128)(2,1)}, bf16[2,2,4,128,512]{4,3,2,1,0:T(8,128)(2,1)}, u32[]{:S(2)}, u32[]{:S(2)}) collective-permute-start(bf16[2,2,4,128,512]{4,3,2,1,0:T(8,128)(2,1)} %pix_weight_half.2), channel_id=1, source_target_pairs={{0,1},{1,0},{2,3},{3,2},{4,5},{5,4},{6,7},{7,6},{8,9},{9,8},{10,11... | collective-permute-start | bytes 6291464 | tf_op jit(solution)/shard_map/ppermute | solution.py:49
  303.1 17.3 %collective-permute-start.23 = (bf16[4,128,256]{2,1,0:T(8,128)(2,1)S(1)}, bf16[4,128,256]{2,1,0:T(8,128)(2,1)S(1)}, u32[]{:S(2)}, u32[]{:S(2)}) collective-permute-start(bf16[4,128,256]{2,1,0:T(8,128)(2,1)S(1)} %dynamic-slice_bitcast_fusion.15), channel_id=1, source_target_pairs={{0,4},{4,0},{8,12},{12,8},{16,20},{20,16},{24,28},{28,24},{1,5},{5... | collective-permute-start | bytes 786440 | tf_op jit(solution)/shard_map/ppermute | solution.py:49
  318.9 26.7 %collective-permute-start.31 = (bf16[2,4,128,512]{3,2,1,0:T(8,128)(2,1)S(1)}, bf16[2,4,128,512]{3,2,1,0:T(8,128)(2,1)S(1)}, u32[]{:S(2)}, u32[]{:S(2)}) collective-permute-start(bf16[2,4,128,512]{3,2,1,0:T(8,128)(2,1)S(1)} %dynamic-slice_bitcast_fusion.6), channel_id=1, source_target_pairs={{0,4},{4,0},{8,12},{12,8},{16,20},{20,16},{24,28},{28,24},{1,5},{5... | collective-permute-start | bytes 3145736 | tf_op jit(solution)/shard_map/ppermute | solution.py:49
  326.4 38.9 %collective-permute-start.27 = (bf16[128,256]{1,0:T(8,128)(2,1)S(1)}, bf16[128,256]{1,0:T(8,128)(2,1)S(1)}, u32[]{:S(2)}, u32[]{:S(2)}) collective-permute-start(bf16[128,256]{1,0:T(8,128)(2,1)S(1)} %get-tuple-element.92), channel_id=1, source_target_pairs={{24,16},{28,20},{25,17},{29,21},{26,18},{30,22},{27,19},{31,23}} | collective-permute-start | bytes 196616 | tf_op jit(solution)/shard_map/ppermute | solution.py:49
  327.1 38.9 %collective-permute-start.25 = (bf16[128,256]{1,0:T(8,128)(2,1)S(1)}, bf16[128,256]{1,0:T(8,128)(2,1)S(1)}, u32[]{:S(2)}, u32[]{:S(2)}) collective-permute-start(bf16[128,256]{1,0:T(8,128)(2,1)S(1)} %fusion.44), channel_id=1, source_target_pairs={{0,8},{8,16},{4,12},{12,20},{1,9},{9,17},{5,13},{13,21},{2,10},{10... | collective-permute-start | bytes 196616 | tf_op jit(solution)/shard_map/ppermute | solution.py:49
  337.9 23.1 %collective-permute-start.49 = (bf16[2,2,128,1024]{3,2,1,0:T(8,128)(2,1)S(1)}, bf16[2,2,128,1024]{3,2,1,0:T(8,128)(2,1)S(1)}, u32[]{:S(2)}, u32[]{:S(2)}) collective-permute-start(bf16[2,2,128,1024]{3,2,1,0:T(8,128)(2,1)S(1)} %get-tuple-element.69), channel_id=1, source_target_pairs={{0,8},{4,12},{1,9},{5,13},{2,10},{6,14},{3,11},{7,15}} | collective-permute-start | bytes 3145736 | tf_op jit(solution)/shard_map/ppermute | solution.py:49
  354.5 65.2 %collective-permute-start.40 = (bf16[2,4,128,1280]{3,2,1,0:T(8,128)(2,1)S(1)}, bf16[2,4,128,1280]{3,2,1,0:T(8,128)(2,1)S(1)}, u32[]{:S(2)}, u32[]{:S(2)}) collective-permute-start(bf16[2,4,128,1280]{3,2,1,0:T(8,128)(2,1)S(1)} %dynamic-slice_bitcast_fusion), channel_id=1, source_target_pairs={{0,2},{2,0},{1,3},{3,1},{4,6},{6,4},{5,7},{7,5},{8,10},{10,8},{9,1... | collective-permute-start | bytes 7864328 | tf_op jit(solution)/shard_map/ppermute | solution.py:49
  360.3 57.9 %collective-permute-start.58 = (bf16[2,4,512,256]{3,2,1,0:T(8,128)(2,1)S(1)}, bf16[2,4,512,256]{3,2,1,0:T(8,128)(2,1)S(1)}, u32[]{:S(2)}, u32[]{:S(2)}) collective-permute-start(bf16[2,4,512,256]{3,2,1,0:T(8,128)(2,1)S(1)} %dynamic-slice_bitcast_fusion.1), channel_id=1, source_target_pairs={{0,4},{4,0},{8,12},{12,8},{16,20},{20,16},{24,28},{28,24},{1,5},{5... | collective-permute-start | bytes 6291464 | tf_op jit(solution)/shard_map/ppermute | solution.py:49
  365.3 46.0 %collective-permute-start.52 = (bf16[2,2,128,1024]{3,2,1,0:T(8,128)(2,1)S(1)}, bf16[2,2,128,1024]{3,2,1,0:T(8,128)(2,1)S(1)}, u32[]{:S(2)}, u32[]{:S(2)}) collective-permute-start(bf16[2,2,128,1024]{3,2,1,0:T(8,128)(2,1)S(1)} %get-tuple-element.70), channel_id=1, source_target_pairs={{24,16},{28,20},{25,17},{29,21},{26,18},{30,22},{27,19},{31,23}} | collective-permute-start | bytes 3145736 | tf_op jit(solution)/shard_map/ppermute | solution.py:49
  367.3 45.2 %collective-permute-start.50 = (bf16[2,2,128,1024]{3,2,1,0:T(8,128)(2,1)S(1)}, bf16[2,2,128,1024]{3,2,1,0:T(8,128)(2,1)S(1)}, u32[]{:S(2)}, u32[]{:S(2)}) collective-permute-start(bf16[2,2,128,1024]{3,2,1,0:T(8,128)(2,1)S(1)} %fusion.6), channel_id=1, source_target_pairs={{0,8},{8,16},{4,12},{12,20},{1,9},{9,17},{5,13},{13,21},{2,10},{10... | collective-permute-start | bytes 3145736 | tf_op jit(solution)/shard_map/ppermute | solution.py:49
  371.8 21.4 %collective-permute-start.34 = (bf16[128,512]{1,0:T(8,128)(2,1)S(1)}, bf16[128,512]{1,0:T(8,128)(2,1)S(1)}, u32[]{:S(2)}, u32[]{:S(2)}) collective-permute-start(bf16[128,512]{1,0:T(8,128)(2,1)S(1)} %fusion.37), channel_id=1, source_target_pairs={{0,8},{8,16},{4,12},{12,20},{1,9},{9,17},{5,13},{13,21},{2,10},{10... | collective-permute-start | bytes 393224 | tf_op jit(solution)/shard_map/ppermute | solution.py:49
  394.7 26.6 %collective-permute-start.26 = (bf16[128,256]{1,0:T(8,128)(2,1)S(1)}, bf16[128,256]{1,0:T(8,128)(2,1)S(1)}, u32[]{:S(2)}, u32[]{:S(2)}) collective-permute-start(bf16[128,256]{1,0:T(8,128)(2,1)S(1)} %get-tuple-element.89), channel_id=1, source_target_pairs={{0,8},{8,16},{16,24},{4,12},{12,20},{20,28},{1,9},{9,17},{17,25},{... | collective-permute-start | bytes 196616 | tf_op jit(solution)/shard_map/ppermute | solution.py:49
  418.2 29.2 %collective-permute-start.53 = (bf16[2,2,128,1024]{3,2,1,0:T(8,128)(2,1)S(1)}, bf16[2,2,128,1024]{3,2,1,0:T(8,128)(2,1)S(1)}, u32[]{:S(2)}, u32[]{:S(2)}) collective-permute-start(bf16[2,2,128,1024]{3,2,1,0:T(8,128)(2,1)S(1)} %get-tuple-element.68), channel_id=1, source_target_pairs={{24,16},{16,8},{28,20},{20,12},{25,17},{17,9},{29,21},{21,13},{26,... | collective-permute-start | bytes 3145736 | tf_op jit(solution)/shard_map/ppermute | solution.py:49
  419.8 25.1 %collective-permute-start.59 = (bf16[4,512,256]{2,1,0:T(8,128)(2,1)S(1)}, bf16[4,512,256]{2,1,0:T(8,128)(2,1)S(1)}, u32[]{:S(2)}, u32[]{:S(2)}) collective-permute-start(bf16[4,512,256]{2,1,0:T(8,128)(2,1)S(1)} %dynamic-slice_bitcast_fusion.3), channel_id=1, source_target_pairs={{0,2},{2,0},{1,3},{3,1},{4,6},{6,4},{5,7},{7,5},{8,10},{10,8},{9,1... | collective-permute-start | bytes 3145736 | tf_op jit(solution)/shard_map/ppermute | solution.py:49
  422.6 51.2 %collective-permute-start.41 = (bf16[4,128,1280]{2,1,0:T(8,128)(2,1)S(1)}, bf16[4,128,1280]{2,1,0:T(8,128)(2,1)S(1)}, u32[]{:S(2)}, u32[]{:S(2)}) collective-permute-start(bf16[4,128,1280]{2,1,0:T(8,128)(2,1)S(1)} %dynamic-slice_bitcast_fusion.2), channel_id=1, source_target_pairs={{0,4},{4,0},{8,12},{12,8},{16,20},{20,16},{24,28},{28,24},{1,5},{5... | collective-permute-start | bytes 3932168 | tf_op jit(solution)/shard_map/ppermute | solution.py:49
  428.9 55.4 %collective-permute-start.51 = (bf16[2,2,128,1024]{3,2,1,0:T(8,128)(2,1)S(1)}, bf16[2,2,128,1024]{3,2,1,0:T(8,128)(2,1)S(1)}, u32[]{:S(2)}, u32[]{:S(2)}) collective-permute-start(bf16[2,2,128,1024]{3,2,1,0:T(8,128)(2,1)S(1)} %get-tuple-element.67), channel_id=1, source_target_pairs={{0,8},{8,16},{16,24},{4,12},{12,20},{20,28},{1,9},{9,17},{17,25},{... | collective-permute-start | bytes 3145736 | tf_op jit(solution)/shard_map/ppermute | solution.py:49
  445.2 24.1 %collective-permute-start.60 = (bf16[512,256]{1,0:T(8,128)(2,1)S(1)}, bf16[512,256]{1,0:T(8,128)(2,1)S(1)}, u32[]{:S(2)}, u32[]{:S(2)}) collective-permute-start(bf16[512,256]{1,0:T(8,128)(2,1)S(1)} %get-tuple-element.81), channel_id=1, source_target_pairs={{0,8},{4,12},{1,9},{5,13},{2,10},{6,14},{3,11},{7,15}} | collective-permute-start | bytes 786440 | tf_op jit(solution)/shard_map/ppermute | solution.py:49
  447.8 36.4 %collective-permute-start.54 = (bf16[2,2,128,1024]{3,2,1,0:T(8,128)(2,1)S(1)}, bf16[2,2,128,1024]{3,2,1,0:T(8,128)(2,1)S(1)}, u32[]{:S(2)}, u32[]{:S(2)}) collective-permute-start(bf16[2,2,128,1024]{3,2,1,0:T(8,128)(2,1)S(1)} %fusion.5), channel_id=1, source_target_pairs={{24,16},{16,8},{8,0},{28,20},{20,12},{12,4},{25,17},{17,9},{9,1},{... | collective-permute-start | bytes 3145736 | tf_op jit(solution)/shard_map/ppermute | solution.py:49
  449.1 27.0 %collective-permute-start.63 = (bf16[512,256]{1,0:T(8,128)(2,1)S(1)}, bf16[512,256]{1,0:T(8,128)(2,1)S(1)}, u32[]{:S(2)}, u32[]{:S(2)}) collective-permute-start(bf16[512,256]{1,0:T(8,128)(2,1)S(1)} %get-tuple-element.82), channel_id=1, source_target_pairs={{24,16},{28,20},{25,17},{29,21},{26,18},{30,22},{27,19},{31,23}} | collective-permute-start | bytes 786440 | tf_op jit(solution)/shard_map/ppermute | solution.py:49
  479.1 26.0 %collective-permute-start.62 = (bf16[512,256]{1,0:T(8,128)(2,1)S(1)}, bf16[512,256]{1,0:T(8,128)(2,1)S(1)}, u32[]{:S(2)}, u32[]{:S(2)}) collective-permute-start(bf16[512,256]{1,0:T(8,128)(2,1)S(1)} %get-tuple-element.79), channel_id=1, source_target_pairs={{0,8},{8,16},{16,24},{4,12},{12,20},{20,28},{1,9},{9,17},{17,25},{... | collective-permute-start | bytes 786440 | tf_op jit(solution)/shard_map/ppermute | solution.py:49
  (58 other events, 496.0 us)
